TPU v7x, 256 devices: a whole 4x4x8 slice. The times are simulated.
256 devices in a mesh: dp: 64 (over x, z, core), ctx: 4 (over y).
Axes of the slice: x: 4, y: 4, z: 8, core: 2. Of those that a mesh axis runs over, the one named last changes fastest.
Arguments:
- queries: bfloat16 [32768, 2048], P(('dp', 'ctx')), may hold values from -100 to 100
- key_rows: bfloat16 [32768, 1024], P(('dp', 'ctx')), may hold values from -6 to 6
- values: bfloat16 [32768, 1024], P(('dp', 'ctx')), may hold values from -6 to 6
- saved_out: bfloat16 [32768, 2048], P(('dp', 'ctx')), may hold values from -6 to 6
- out_grad: bfloat16 [32768, 2048], P(('dp', 'ctx')), may hold values from -6 to 6
- pack_of: int32 [32768, 1], P(('dp', 'ctx')), may hold values from 0 to 63; in each aligned block of 128 rows (0 to 127, 128 to 255, ...) at most 3 rows name the same one
- segment_label: int32 [32768], P(('dp', 'ctx')), may hold values from 0 to 3
Outputs:
- grad_queries: bfloat16 [32768, 2048], P(('dp', 'ctx'))
- grad_keys: bfloat16 [32768, 1024], P(('dp', 'ctx'))
- grad_values: bfloat16 [32768, 1024], P(('dp', 'ctx'))
Inputs may be any that keep to these rules, and one draw needn't show every extreme that they name: `pack_of`: the 128 rows of one device name each pack at most 3 times, a bound that some block reaches.
All inputs are finite; a program needn't handle non-finite values.
Results may differ from a plain program's by a relative error of at most 0.013.
Values may be sent and summed in bfloat16 or wider, within the bound.
A program may use at most 64 MiB of HBM per device.

v0:
```python
import math

import jax
import jax.numpy as jnp
from jax import lax
from jax.sharding import PartitionSpec as P

HD = 256


MASKED = -1e30


def device_ranks(target, dest_count):
    onehot = (target[:, None] == jnp.arange(dest_count, dtype=jnp.int32)[None, :]).astype(jnp.int32)
    before = jnp.cumsum(onehot, axis=0) - onehot
    return jnp.sum(before * onehot, axis=1)


def row_products(grad_rows, out_rows, head_count):
    product = grad_rows.astype(jnp.float32) * out_rows.astype(jnp.float32)
    return jnp.sum(product.reshape(product.shape[0], head_count, HD), axis=2).astype(jnp.bfloat16)


def attend(
    query_rows, grad_rows, delta_rows, query_label, key_head, value_head, key_label, score_scale
):
    scores = (
        jnp.einsum("rgd,kd->grk", query_rows, key_head, preferred_element_type=jnp.float32)
        * score_scale
    )
    allowed = (query_label[:, None] == key_label[None, :]) & (key_label[None, :] > 0.5)
    scores = jnp.where(allowed[None], scores, MASKED)
    row_max = jnp.max(scores, axis=2, keepdims=True)
    logsum = row_max + jnp.log(jnp.sum(jnp.exp(scores - row_max), axis=2, keepdims=True))
    probs_full = jnp.exp(scores - logsum)
    dprobs = jnp.einsum("rgd,kd->grk", grad_rows, value_head, preferred_element_type=jnp.float32)
    offset = jnp.transpose(delta_rows.astype(jnp.float32))[:, :, None]
    dscore = (probs_full * (dprobs - offset) * score_scale).astype(jnp.bfloat16)
    return (probs_full.astype(jnp.bfloat16), dscore, logsum)


def body(queries, key_rows, values, saved_out, out_grad, pack_of, segment_label):
    pack_count = lax.axis_size("dp")
    row_count = queries.shape[0]
    capacity = row_count // pack_count + max(1, row_count // (4 * pack_count))
    slots = pack_count * capacity
    q_heads = queries.shape[1] // HD
    k_heads = key_rows.shape[1] // HD
    group_size = q_heads // k_heads
    score_scale = 1.0 / math.sqrt(HD)
    target = pack_of[:, 0]
    position = target * capacity + device_ranks(target, pack_count)

    def to_slots(matrix):
        return jnp.zeros((slots,) + matrix.shape[1:], matrix.dtype).at[position].set(matrix)

    labels = to_slots((segment_label + 1).astype(jnp.bfloat16))
    row_delta = row_products(out_grad, saved_out, q_heads)
    got_q, got_k, got_v, got_g, got_d, got_l = (
        lax.all_to_all(to_slots(queries), "dp", split_axis=0, concat_axis=0, tiled=True),
        lax.all_to_all(to_slots(key_rows), "dp", split_axis=0, concat_axis=0, tiled=True),
        lax.all_to_all(to_slots(values), "dp", split_axis=0, concat_axis=0, tiled=True),
        lax.all_to_all(to_slots(out_grad), "dp", split_axis=0, concat_axis=0, tiled=True),
        lax.all_to_all(to_slots(row_delta), "dp", split_axis=0, concat_axis=0, tiled=True),
        lax.all_to_all(labels, "dp", split_axis=0, concat_axis=0, tiled=True),
    )
    all_k, all_v, all_l = (
        lax.all_gather(got_k, "ctx", axis=0, tiled=True),
        lax.all_gather(got_v, "ctx", axis=0, tiled=True),
        lax.all_gather(got_l, "ctx", axis=0, tiled=True),
    )
    grad_q_heads = []
    key_terms = []
    value_terms = []
    for head in range(k_heads):
        qcols = slice(head * group_size * HD, (head + 1) * group_size * HD)
        kcols = slice(head * HD, (head + 1) * HD)
        query_rows = got_q[:, qcols].reshape(slots, group_size, HD)
        grad_rows = got_g[:, qcols].reshape(slots, group_size, HD)
        delta_rows = got_d[:, head * group_size : (head + 1) * group_size]
        key_head = all_k[:, kcols]
        weights, dscore, logsum = attend(
            query_rows, grad_rows, delta_rows, got_l, key_head, all_v[:, kcols], all_l, score_scale
        )
        grad_q_heads.append(
            jnp.einsum("grk,kd->rgd", dscore, key_head, preferred_element_type=jnp.float32).reshape(
                slots, group_size * HD
            )
        )
        key_terms.append(
            jnp.einsum("grk,rgd->kd", dscore, query_rows, preferred_element_type=jnp.float32)
        )
        value_terms.append(
            jnp.einsum("grk,rgd->kd", weights, grad_rows, preferred_element_type=jnp.float32)
        )
    grad_q = jnp.concatenate(grad_q_heads, axis=1).astype(jnp.bfloat16)
    summed_k, summed_v = (
        lax.psum_scatter(
            jnp.concatenate(key_terms, axis=1).astype(jnp.bfloat16),
            "ctx",
            scatter_dimension=0,
            tiled=True,
        ).astype(jnp.float32),
        lax.psum_scatter(
            jnp.concatenate(value_terms, axis=1).astype(jnp.bfloat16),
            "ctx",
            scatter_dimension=0,
            tiled=True,
        ).astype(jnp.float32),
    )
    grad_k = summed_k.astype(jnp.bfloat16)
    grad_v = summed_v.astype(jnp.bfloat16)
    back_q, back_k, back_v = (
        lax.all_to_all(grad_q, "dp", split_axis=0, concat_axis=0, tiled=True),
        lax.all_to_all(grad_k, "dp", split_axis=0, concat_axis=0, tiled=True),
        lax.all_to_all(grad_v, "dp", split_axis=0, concat_axis=0, tiled=True),
    )
    return (back_q[position], back_k[position], back_v[position])


def solution(mesh):
    return jax.shard_map(
        body,
        mesh=mesh,
        in_specs=(
            P(("dp", "ctx"), None),
            P(("dp", "ctx"), None),
            P(("dp", "ctx"), None),
            P(("dp", "ctx"), None),
            P(("dp", "ctx"), None),
            P(("dp", "ctx"), None),
            P(("dp", "ctx")),
        ),
        out_specs=(P(("dp", "ctx"), None), P(("dp", "ctx"), None), P(("dp", "ctx"), None)),
        check_vma=False,
    )
```

profile of v0, /device:TPU:1, one launch (start us, length us, event | category | flops | bytes accessed | tf_op | source)
XLA Modules:
  0.0 290.8 jit_solution(12971251816439714753)
XLA Ops:
  10.2 1.3 scatter_custom_fusion.1
  12.4 13.0 %all-to-all-start.1 = ((bf16[64,3,1]{1,2,0:T(2,128)(2,1)}), bf16[64,3,1]{1,2,0:T(2,128)(2,1)S(1)}, u32[]{:S(2)}, u32[]{:S(2)}) async-start(bf16[64,3,1]{1,2,0:T(2,128)(2,1)} %all_to_all.93), calls=%async_computation.1 | async-start | bytes 65536 | tf_op jit(solution)/shard_map/all_to_all | solution.py:66
  25.4 1.3 convert_multiply_fusion
  28.8 5.8 %all-to-all-done.1 = bf16[64,3,1]{1,2,0:T(2,128)(2,1)S(1)} async-done(((bf16[64,3,1]{1,2,0:T(2,128)(2,1)}), bf16[64,3,1]{1,2,0:T(2,128)(2,1)S(1)}, u32[]{:S(2)}, u32[]{:S(2)}) %all-to-all-start.1) | async-done | bytes 416 | tf_op jit(solution)/shard_map/all_to_all | solution.py:66
  34.6 4.7 %all-to-all-start.5 = ((bf16[64,3,8]{2,1,0:T(4,128)(2,1)}), bf16[64,3,8]{2,1,0:T(4,128)(2,1)S(1)}, u32[]{:S(2)}, u32[]{:S(2)}) async-start(bf16[64,3,8]{2,1,0:T(4,128)(2,1)} %all_to_all.82), calls=%async_computation.5 | async-start | bytes 131072 | tf_op jit(solution)/shard_map/all_to_all | solution.py:65
  39.3 1.7 scatter_custom_fusion
  41.0 1.0 all_to_all.68
  42.0 7.2 %all-to-all-done.5 = bf16[64,3,8]{2,1,0:T(4,128)(2,1)S(1)} async-done(((bf16[64,3,8]{2,1,0:T(4,128)(2,1)}), bf16[64,3,8]{2,1,0:T(4,128)(2,1)S(1)}, u32[]{:S(2)}, u32[]{:S(2)}) %all-to-all-start.5) | async-done | bytes 3104 | tf_op jit(solution)/shard_map/all_to_all | solution.py:65
  49.2 4.5 %all-to-all-start = ((bf16[64,3,1024]{2,1,0:T(4,128)(2,1)}), bf16[64,3,1024]{2,1,0:T(4,128)(2,1)S(1)}, u32[]{:S(2)}, u32[]{:S(2)}) async-start(bf16[64,3,1024]{2,1,0:T(4,128)(2,1)} %all_to_all.68), calls=%async_computation | async-start | bytes 1048576 | tf_op jit(solution)/shard_map/all_to_all | solution.py:62
  53.7 1.7 scatter_custom_fusion.3
  55.3 1.0 all_to_all.76
  56.4 14.6 %all-to-all-done = bf16[64,3,1024]{2,1,0:T(4,128)(2,1)S(1)} async-done(((bf16[64,3,1024]{2,1,0:T(4,128)(2,1)}), bf16[64,3,1024]{2,1,0:T(4,128)(2,1)S(1)}, u32[]{:S(2)}, u32[]{:S(2)}) %all-to-all-start) | async-done | bytes 393248 | tf_op jit(solution)/shard_map/all_to_all | solution.py:62
  71.0 6.4 %all-to-all-start.3 = ((bf16[64,3,1024]{2,1,0:T(4,128)(2,1)}), bf16[64,3,1024]{2,1,0:T(4,128)(2,1)S(1)}, u32[]{:S(2)}, u32[]{:S(2)}) async-start(bf16[64,3,1024]{2,1,0:T(4,128)(2,1)} %all_to_all.76), calls=%async_computation.3 | async-start | bytes 1048576 | tf_op jit(solution)/shard_map/all_to_all | solution.py:63
  77.4 1.1 all_to_all.70
  78.5 2.1 scatter_custom_fusion.4
  80.7 1.3 all_to_all.79
  81.9 12.8 %all-to-all-done.3 = bf16[64,3,1024]{2,1,0:T(4,128)(2,1)S(1)} async-done(((bf16[64,3,1024]{2,1,0:T(4,128)(2,1)}), bf16[64,3,1024]{2,1,0:T(4,128)(2,1)S(1)}, u32[]{:S(2)}, u32[]{:S(2)}) %all-to-all-start.3) | async-done | bytes 393248 | tf_op jit(solution)/shard_map/all_to_all | solution.py:63
  94.7 6.3 %all-to-all-start.4 = ((bf16[64,3,2048]{2,1,0:T(4,128)(2,1)}), bf16[64,3,2048]{2,1,0:T(4,128)(2,1)S(1)}, u32[]{:S(2)}, u32[]{:S(2)}) async-start(bf16[64,3,2048]{2,1,0:T(4,128)(2,1)} %all_to_all.79), calls=%async_computation.4 | async-start | bytes 2097152 | tf_op jit(solution)/shard_map/all_to_all | solution.py:64
  101.0 2.1 scatter_custom_fusion.2
  103.1 1.3 all_to_all.73
  104.4 25.1 %all-to-all-done.4 = bf16[64,3,2048]{2,1,0:T(4,128)(2,1)S(1)} async-done(((bf16[64,3,2048]{2,1,0:T(4,128)(2,1)}), bf16[64,3,2048]{2,1,0:T(4,128)(2,1)S(1)}, u32[]{:S(2)}, u32[]{:S(2)}) %all-to-all-start.4) | async-done | bytes 786464 | tf_op jit(solution)/shard_map/all_to_all | solution.py:64
  129.6 6.2 %all-to-all-start.2 = ((bf16[64,3,2048]{2,1,0:T(4,128)(2,1)}), bf16[64,3,2048]{2,1,0:T(4,128)(2,1)S(1)}, u32[]{:S(2)}, u32[]{:S(2)}) async-start(bf16[64,3,2048]{2,1,0:T(4,128)(2,1)} %all_to_all.73), calls=%async_computation.2 | async-start | bytes 2097152 | tf_op jit(solution)/shard_map/all_to_all | solution.py:61
  135.8 1.1 all_to_all.78
  138.7 9.3 %all-reduce = bf16[768]{0:T(1024)(128)(2,1)S(1)} all-reduce(bf16[768]{0:T(1024)(128)(2,1)S(1)} %dynamic-update-slice), channel_id=1, replica_groups=mesh['dp'=64,'ctx'=4] {'ctx'}, use_global_device_ids=true, to_apply=%add | all-reduce | flops 768 | bytes 3072
  150.0 14.3 %all-to-all-done.2 = bf16[64,3,2048]{2,1,0:T(4,128)(2,1)S(1)} async-done(((bf16[64,3,2048]{2,1,0:T(4,128)(2,1)}), bf16[64,3,2048]{2,1,0:T(4,128)(2,1)S(1)}, u32[]{:S(2)}, u32[]{:S(2)}) %all-to-all-start.2) | async-done | bytes 786464 | tf_op jit(solution)/shard_map/all_to_all | solution.py:61
  165.8 1.5 fusion.97
  167.8 0.9 all-gather.5.cloned.1.call-done
  168.7 1.5 fusion.23
  178.5 1.6 copy.65
  184.7 1.6 copy.67
  186.4 1.0 copy-done.9
  187.4 1.3 fusion.35
  188.8 1.4 fusion.32
  190.9 1.4 fusion.34
  192.6 1.3 fusion.33
  194.3 1.6 pad_maximum_fusion.2
  195.9 10.7 %all-to-all-start.6 = ((bf16[64,3,2048]{2,1,0:T(4,128)(2,1)}), bf16[64,3,2048]{2,1,0:T(4,128)(2,1)S(1)}, u32[]{:S(2)}, u32[]{:S(2)}) async-start(bf16[64,3,2048]{2,1,0:T(4,128)(2,1)} %pad_maximum_fusion.2), calls=%async_computation.6 | async-start | bytes 2097152 | tf_op jit(solution)/shard_map/all_to_all | solution.py:115
  206.6 1.1 reduce-scatter.7.cloned.1.call-done
  207.7 2.1 all_to_all.87
  209.8 25.4 %all-to-all-done.6 = bf16[64,3,2048]{2,1,0:T(4,128)(2,1)S(1)} async-done(((bf16[64,3,2048]{2,1,0:T(4,128)(2,1)}), bf16[64,3,2048]{2,1,0:T(4,128)(2,1)S(1)}, u32[]{:S(2)}, u32[]{:S(2)}) %all-to-all-start.6) | async-done | bytes 786464 | tf_op jit(solution)/shard_map/all_to_all | solution.py:115
  235.2 6.2 %all-to-all-start.7 = ((bf16[64,3,1024]{2,1,0:T(4,128)(2,1)}), bf16[64,3,1024]{2,1,0:T(4,128)(2,1)S(1)}, u32[]{:S(2)}, u32[]{:S(2)}) async-start(bf16[64,3,1024]{2,1,0:T(4,128)(2,1)} %all_to_all.87), calls=%async_computation.7 | async-start | bytes 1048576 | tf_op jit(solution)/shard_map/all_to_all | solution.py:116
  241.4 2.1 all_to_all.90
  243.5 15.2 %all-to-all-done.7 = bf16[64,3,1024]{2,1,0:T(4,128)(2,1)S(1)} async-done(((bf16[64,3,1024]{2,1,0:T(4,128)(2,1)}), bf16[64,3,1024]{2,1,0:T(4,128)(2,1)S(1)}, u32[]{:S(2)}, u32[]{:S(2)}) %all-to-all-start.7) | async-done | bytes 393248 | tf_op jit(solution)/shard_map/all_to_all | solution.py:116
  258.7 6.3 %all-to-all-start.8 = ((bf16[64,3,1024]{2,1,0:T(4,128)(2,1)}), bf16[64,3,1024]{2,1,0:T(4,128)(2,1)S(1)}, u32[]{:S(2)}, u32[]{:S(2)}) async-start(bf16[64,3,1024]{2,1,0:T(4,128)(2,1)} %all_to_all.90), calls=%async_computation.8 | async-start | bytes 1048576 | tf_op jit(solution)/shard_map/all_to_all | solution.py:117
  265.7 1.7 gather_fusion
  267.8 1.6 gather_fusion.1
  269.3 13.0 %all-to-all-done.8 = bf16[64,3,1024]{2,1,0:T(4,128)(2,1)S(1)} async-done(((bf16[64,3,1024]{2,1,0:T(4,128)(2,1)}), bf16[64,3,1024]{2,1,0:T(4,128)(2,1)S(1)}, u32[]{:S(2)}, u32[]{:S(2)}) %all-to-all-start.8) | async-done | bytes 393248 | tf_op jit(solution)/shard_map/all_to_all | solution.py:117
  282.7 1.6 gather_fusion.2
  (112 shorter events, 26.4 us)
Async XLA Ops:
  12.4 22.2 %all-to-all-start.1 = ((bf16[64,3,1]{1,2,0:T(2,128)(2,1)}), bf16[64,3,1]{1,2,0:T(2,128)(2,1)S(1)}, u32[]{:S(2)}, u32[]{:S(2)}) async-start(bf16[64,3,1]{1,2,0:T(2,128)(2,1)} %all_to_all.93), calls=%async_computation.1 | async-start | bytes 65536 | tf_op jit(solution)/shard_map/all_to_all | solution.py:66
  34.6 14.6 %all-to-all-start.5 = ((bf16[64,3,8]{2,1,0:T(4,128)(2,1)}), bf16[64,3,8]{2,1,0:T(4,128)(2,1)S(1)}, u32[]{:S(2)}, u32[]{:S(2)}) async-start(bf16[64,3,8]{2,1,0:T(4,128)(2,1)} %all_to_all.82), calls=%async_computation.5 | async-start | bytes 131072 | tf_op jit(solution)/shard_map/all_to_all | solution.py:65
  49.2 21.8 %all-to-all-start = ((bf16[64,3,1024]{2,1,0:T(4,128)(2,1)}), bf16[64,3,1024]{2,1,0:T(4,128)(2,1)S(1)}, u32[]{:S(2)}, u32[]{:S(2)}) async-start(bf16[64,3,1024]{2,1,0:T(4,128)(2,1)} %all_to_all.68), calls=%async_computation | async-start | bytes 1048576 | tf_op jit(solution)/shard_map/all_to_all | solution.py:62
  71.0 23.7 %all-to-all-start.3 = ((bf16[64,3,1024]{2,1,0:T(4,128)(2,1)}), bf16[64,3,1024]{2,1,0:T(4,128)(2,1)S(1)}, u32[]{:S(2)}, u32[]{:S(2)}) async-start(bf16[64,3,1024]{2,1,0:T(4,128)(2,1)} %all_to_all.76), calls=%async_computation.3 | async-start | bytes 1048576 | tf_op jit(solution)/shard_map/all_to_all | solution.py:63
  77.4 88.5 %all-gather.3.cloned.1.call-start = ((), (), s32[]{:S(2)}) async-start(), calls=%async_computation.11 | async-start | bytes 1966080 | tf_op jit(solution)/shard_map/all_gather | solution.py:69
  94.7 34.8 %all-to-all-start.4 = ((bf16[64,3,2048]{2,1,0:T(4,128)(2,1)}), bf16[64,3,2048]{2,1,0:T(4,128)(2,1)S(1)}, u32[]{:S(2)}, u32[]{:S(2)}) async-start(bf16[64,3,2048]{2,1,0:T(4,128)(2,1)} %all_to_all.79), calls=%async_computation.4 | async-start | bytes 2097152 | tf_op jit(solution)/shard_map/all_to_all | solution.py:64
  129.6 34.8 %all-to-all-start.2 = ((bf16[64,3,2048]{2,1,0:T(4,128)(2,1)}), bf16[64,3,2048]{2,1,0:T(4,128)(2,1)S(1)}, u32[]{:S(2)}, u32[]{:S(2)}) async-start(bf16[64,3,2048]{2,1,0:T(4,128)(2,1)} %all_to_all.73), calls=%async_computation.2 | async-start | bytes 2097152 | tf_op jit(solution)/shard_map/all_to_all | solution.py:61
  135.8 1.2 copy-start.19
  135.8 32.9 %all-gather.5.cloned.1.call-start = ((), (), s32[]{:S(2)}) async-start(), calls=%async_computation.12 | async-start | bytes 1966080 | tf_op jit(solution)/shard_map/all_gather | solution.py:70
  136.9 70.8 %reduce-scatter.7.cloned.1.call-start = ((), (), s32[]{:S(2)}) async-start(), calls=%async_computation.13 | async-start | bytes 1966080 | tf_op jit(solution)/shard_map/reduce_scatter | solution.py:99
  167.4 1.3 copy-start.6
  168.7 2.0 copy-start.17
  170.2 1.6 copy-start.8
  170.2 1.1 copy-start.16
  171.3 1.4 copy-start.18
  171.8 1.3 copy-start
  173.1 0.9 copy-start.10
  174.1 1.0 copy-start.2
  175.1 0.9 copy-start.12
  176.0 1.0 copy-start.4
  177.1 0.9 copy-start.14
  180.1 0.9 copy-start.7
  180.1 1.4 copy-start.1
  180.1 61.3 %reduce-scatter.9.cloned.1.call-start = ((), (), s32[]{:S(2)}) async-start(), calls=%async_computation.14 | async-start | bytes 1966080 | tf_op jit(solution)/shard_map/reduce_scatter | solution.py:105
  181.6 1.3 copy-start.3
  182.8 1.3 copy-start.5
  186.3 1.1 copy-start.9
  186.3 2.4 copy-start.11
  188.7 2.1 copy-start.13
  190.7 1.9 copy-start.15
  195.9 39.3 %all-to-all-start.6 = ((bf16[64,3,2048]{2,1,0:T(4,128)(2,1)}), bf16[64,3,2048]{2,1,0:T(4,128)(2,1)S(1)}, u32[]{:S(2)}, u32[]{:S(2)}) async-start(bf16[64,3,2048]{2,1,0:T(4,128)(2,1)} %pad_maximum_fusion.2), calls=%async_computation.6 | async-start | bytes 2097152 | tf_op jit(solution)/shard_map/all_to_all | solution.py:115
  235.2 23.5 %all-to-all-start.7 = ((bf16[64,3,1024]{2,1,0:T(4,128)(2,1)}), bf16[64,3,1024]{2,1,0:T(4,128)(2,1)S(1)}, u32[]{:S(2)}, u32[]{:S(2)}) async-start(bf16[64,3,1024]{2,1,0:T(4,128)(2,1)} %all_to_all.87), calls=%async_computation.7 | async-start | bytes 1048576 | tf_op jit(solution)/shard_map/all_to_all | solution.py:116
  258.7 23.6 %all-to-all-start.8 = ((bf16[64,3,1024]{2,1,0:T(4,128)(2,1)}), bf16[64,3,1024]{2,1,0:T(4,128)(2,1)S(1)}, u32[]{:S(2)}, u32[]{:S(2)}) async-start(bf16[64,3,1024]{2,1,0:T(4,128)(2,1)} %all_to_all.90), calls=%async_computation.8 | async-start | bytes 1048576 | tf_op jit(solution)/shard_map/all_to_all | solution.py:117
Sparse Core Ops, SparseCore 0:
  80.6 30.2 all-gather.2
  138.4 30.2 all-gather.4
  180.2 27.4 reduce-scatter.6
  210.1 27.9 reduce-scatter.8
where the time goes:
time: 292 us; the launch traced here: 291 us
  waiting for transfers between devices  135 us (46%)
  starting transfers between devices  64.6 us (22%)
  local copies, waits for them, and re-layouts  41.8 us (14%)
  between operations  15 us (5%)
  matrix products  14.8 us (5%)
  other arithmetic  9.79 us (3%)
  blocking collectives  9.29 us (3%)
    all_to_all x1, waiting for transfers between devices, body(): lax.all_to_all(grad_q, 'dp', split_axis=0, concat_axis=0, tiled=True)  25.4 us
    all_to_all x1, waiting for transfers between devices, body(): lax.all_to_all(to_slots(out_grad), 'dp', split_axis=0, concat_axis=0, til...  25.1 us
    all_to_all x1, waiting for transfers between devices, body(): lax.all_to_all(grad_k, 'dp', split_axis=0, concat_axis=0, tiled=True)  15.2 us
    all_to_all x1, waiting for transfers between devices, body(): lax.all_to_all(to_slots(key_rows), 'dp', split_axis=0, concat_axis=0, til...  14.6 us
    all_to_all x1, waiting for transfers between devices, body(): lax.all_to_all(to_slots(queries), 'dp', split_axis=0, concat_axis=0, tile...  14.3 us
    all_to_all x1, starting transfers between devices, body(): lax.all_to_all(labels, 'dp', split_axis=0, concat_axis=0, tiled=True)  13 us
    all_to_all x1, waiting for transfers between devices, body(): lax.all_to_all(grad_v, 'dp', split_axis=0, concat_axis=0, tiled=True)  13 us
    all_to_all x1, waiting for transfers between devices, body(): lax.all_to_all(to_slots(values), 'dp', split_axis=0, concat_axis=0, tiled...  12.8 us
  transfers between devices with their start and end apart: 13, of which 11 were waited for; matrix products, arithmetic and copies ran while one was open for 11% of the time, Pallas kernels for 0%

commit v1 on v0

v1 whole, which is shorter than its diff:
```python
import jax
import jax.numpy as jnp
from jax import lax
from jax.experimental import pallas as pl
from jax.experimental.pallas import tpu as pltpu
from jax.sharding import PartitionSpec as P

MESH = pl.DeviceIdType.MESH
F32 = jnp.float32
BF16 = jnp.bfloat16

NDP = 64
NY = 4
TOK = 128
CAP = 3
HD = 256
SLOT = NY * CAP
ROWS = NDP * SLOT
GRP = 8
MASKED = -1e30
SCALE = 1.0 / 16.0

NT, NB = 6, 4


def iota(shape, dim):
    return lax.broadcasted_iota(jnp.int32, shape, dim)


def mm(a, b, ca, cb):
    return lax.dot_general(a, b, (((ca,), (cb,)), ((), ())), preferred_element_type=F32)


def partner(i, x, z, c):
    nx = lax.rem(x + i // 16, 4)
    nz = lax.rem(z + lax.rem(i // 2, 8), 8)
    nc = lax.rem(c + i, 2)
    return (nx * 8 + nz) * 2 + nc


def kernel(
    q_ref, k_ref, v_ref, g_ref, o_ref, pcol_ref, prow_ref, lab_ref,
    oq_ref, ok_ref, ov_ref,
    tok, meta_s, meta_r, place, gather, fsend, frecv, msend, mrecv, xs, rowv, labk,
    dq_acc, dk_acc, dv_acc, bsend, brecv, obuf,
    ysend, yrecv, ymsend, ymrecv, zsend, zrecv, zmsend, zmrecv, bsem_s, bsem_r, osem_s, osem_r,
):
    dp = lax.axis_index("dp")
    y = lax.axis_index("ctx")
    x, z, c = dp // 16, lax.rem(dp // 2, 8), lax.rem(dp, 2)
    bar = pltpu.get_barrier_semaphore()

    def greet(i, carry):
        pl.semaphore_signal(bar, inc=1, device_id=(partner(i, x, z, c), y), device_id_type=MESH)
        return carry

    lax.fori_loop(1, NDP, greet, 0)
    for dy in range(1, NY):
        pl.semaphore_signal(bar, inc=1, device_id=(dp, lax.rem(y + dy, NY)), device_id_type=MESH)

    pcol = pcol_ref[...]
    prow = prow_ref[...]
    earlier = (pcol == prow) & (iota((TOK, TOK), 0) < iota((TOK, TOK), 1))
    rank = jnp.sum(earlier.astype(F32), axis=0, keepdims=True)
    slot = rank + (y * CAP).astype(F32)
    lab = lab_ref[...].astype(F32) + 1.0

    prod = g_ref[...].astype(F32) * o_ref[...].astype(F32)
    hi = prod.astype(BF16)
    lo = (prod - hi.astype(F32)).astype(BF16)
    pick = (iota((8, 8 * HD), 1) // HD == iota((8, 8 * HD), 0)).astype(BF16)
    delta = (mm(pick, hi, 1, 1) + mm(pick, lo, 1, 1)).astype(BF16).astype(F32)
    for t in range(NY):
        meta_s[t, 0:1, :] = prow.astype(F32)
        meta_s[t, 1:2, :] = slot
        meta_s[t, 2:3, :] = lab
        meta_s[t, 3:5, :] = delta[2 * t : 2 * t + 2, :]
        meta_s[t, 5:8, :] = jnp.zeros((3, TOK), F32)
    meta_r[y] = meta_s[y]

    pl.semaphore_wait(bar, NDP - 1 + NY - 1)

    def columns(kind, head):
        if kind == 0:
            return k_ref.at[:, pl.ds(pl.multiple_of(head * HD, HD), HD)]
        if kind == 1:
            return v_ref.at[:, pl.ds(pl.multiple_of(head * HD, HD), HD)]
        ref = q_ref if kind % 2 == 0 else g_ref
        return ref.at[:, pl.ds(pl.multiple_of(head * 2 * HD + (kind // 2 - 1) * HD, HD), HD)]

    for dy in range(1, NY):
        t = lax.rem(y + dy, NY)
        pltpu.make_async_remote_copy(
            src_ref=meta_s.at[t], dst_ref=meta_r.at[y], send_sem=ymsend, recv_sem=ymrecv,
            device_id=(dp, t), device_id_type=MESH,
        ).start()
    for kind in range(NT):
        for dy in range(1, NY):
            t = lax.rem(y + dy, NY)
            pltpu.make_async_remote_copy(
                src_ref=columns(kind, t), dst_ref=tok.at[kind, y], send_sem=ysend, recv_sem=yrecv.at[kind // 2],
                device_id=(dp, t), device_id_type=MESH,
            ).start()
        pltpu.make_async_copy(columns(kind, y), tok.at[kind, y], yrecv.at[kind // 2]).start()

    pltpu.make_async_copy(meta_s.at[pl.ds(0, NY - 1)], meta_r.at[pl.ds(0, NY - 1)], ymrecv).wait()
    packs = jnp.concatenate([meta_r[t, 0:1, :] for t in range(NY)], axis=1)
    slots = jnp.concatenate([meta_r[t, 1:2, :] for t in range(NY)], axis=1)
    where = (packs * (2.0 * SLOT) + slots).astype(jnp.int32)

    def place_block(b, carry):
        r = iota((HD, NY * TOK), 0) + b * HD
        at = pl.ds(pl.multiple_of(b * HD, HD), HD)
        place[at, 0 : NY * TOK] = (r == where).astype(F32).astype(BF16)
        place[at, NY * TOK : 2 * NY * TOK] = (r == where + SLOT).astype(F32).astype(BF16)
        return carry

    lax.fori_loop(0, 2 * ROWS // HD, place_block, 0)

    owner = (iota((NDP, NY * TOK), 0).astype(F32) == packs).astype(F32).astype(BF16)
    lane = iota((128, NY * TOK), 0)
    vals = [jnp.concatenate([meta_r[t, 2 + j : 3 + j, :] for t in range(NY)], axis=1) for j in range(3)]
    kindv = jnp.where(lane // 16 == 0, vals[0], jnp.where(lane // 16 == 1, vals[1], vals[2]))
    hit = (lax.rem(lane, 16).astype(F32) == slots) & (lane < 48)
    small = jnp.where(hit, kindv, 0.0).astype(BF16)
    msend[...] = mm(owner, small, 1, 1).reshape(NDP, 1, 128)

    def meta_out(i, carry):
        d = partner(i, x, z, c)
        pltpu.make_async_remote_copy(
            src_ref=msend.at[d], dst_ref=mrecv.at[dp], send_sem=zmsend, recv_sem=zmrecv,
            device_id=(d, y), device_id_type=MESH,
        ).start()
        return carry

    for chunk in range(3):
        both = pl.ds(2 * chunk, 2)
        pltpu.make_async_copy(tok.at[both], tok.at[both], yrecv.at[chunk]).wait()
        for j in range(2):
            t = tok[2 * chunk + j].reshape(NY * TOK, HD)
            halves = jnp.concatenate([t[:, 0:128], t[:, 128:256]], axis=0)

            def fill(b, carry):
                got = mm(place[pl.ds(pl.multiple_of(b * 192, 192), 192), :], halves, 1, 0)
                fsend[chunk, pl.ds(b * GRP, GRP), 3 * j : 3 * j + 3] = got.astype(BF16).reshape(GRP, 3, 8, 128)
                return carry

            lax.fori_loop(0, NDP // GRP, fill, 0)

        def out(i, carry):
            d = partner(i, x, z, c)
            pltpu.make_async_remote_copy(
                src_ref=fsend.at[chunk, d], dst_ref=frecv.at[chunk, dp], send_sem=zsend, recv_sem=zrecv.at[chunk],
                device_id=(d, y), device_id_type=MESH,
            ).start()
            return carry

        lax.fori_loop(1, NDP, out, 0)
        pltpu.make_async_copy(fsend.at[chunk, dp], frecv.at[chunk, dp], zrecv.at[chunk]).start()
        if chunk == 0:
            lax.fori_loop(1, NDP, meta_out, 0)
            pltpu.make_async_copy(msend.at[dp], mrecv.at[dp], zmrecv).start()

    eye = (iota((TOK, TOK), 0) == iota((TOK, TOK), 1)).astype(F32).astype(BF16)
    for t in range(NY):
        col = mm(eye, meta_r[t].astype(BF16), 1, 1)
        home = (col[:, 0:1] * (2.0 * SLOT) + col[:, 1:2]).astype(jnp.int32)
        for half in range(2):
            row = half * NY * TOK + t * TOK

            def gather_block(b, carry):
                r = iota((TOK, HD), 1) + b * HD
                gather[row : row + TOK, pl.ds(pl.multiple_of(b * HD, HD), HD)] = (
                    (r == home + half * SLOT).astype(F32).astype(BF16)
                )
                return carry

            lax.fori_loop(0, 2 * ROWS // HD, gather_block, 0)

    a, b = iota((192, 192), 0), iota((192, 192), 1)
    split = (b == (lax.rem(a, 96) // 12) * 24 + (a // 96) * 12 + lax.rem(a, 12)).astype(F32).astype(BF16)
    join = (a == (lax.rem(b, 96) // 12) * 24 + (b // 96) * 12 + lax.rem(b, 12)).astype(F32).astype(BF16)

    pltpu.make_async_copy(mrecv, mrecv, zmrecv).wait()
    spread = (iota((ROWS, NDP), 0) // SLOT == iota((ROWS, NDP), 1)).astype(F32).astype(BF16)
    rows = mm(spread, mrecv[...].reshape(NDP, 128).astype(BF16), 1, 0)
    r12, l128 = lax.rem(iota((ROWS, 128), 0), SLOT), iota((ROWS, 128), 1)
    own = jnp.where((lax.rem(l128, 16) == r12) & (l128 < 48), rows, 0.0)
    labcol = jnp.sum(jnp.where(l128 < 16, own, 0.0), axis=1, keepdims=True)
    labk[...] = jnp.broadcast_to(jnp.where(labcol > 0.5, labcol, -1.0), (ROWS, 128))
    pick16 = (iota((8, 128), 1) // 16 == iota((8, 128), 0)).astype(F32).astype(BF16)
    rowv[...] = mm(pick16, own.astype(BF16), 1, 1)

    def take(chunk):
        pltpu.make_async_copy(frecv.at[chunk], frecv.at[chunk], zrecv.at[chunk]).wait()

        def unmix(b, carry):
            for j in range(2):
                block = frecv[chunk, pl.ds(b * GRP, GRP), 3 * j : 3 * j + 3].reshape(192, 128)
                got = mm(split, block, 1, 0).astype(BF16)
                at = pl.ds(pl.multiple_of(b * 96, 96), 96)
                xs[2 * chunk + j, at, 0:128] = got[0:96]
                xs[2 * chunk + j, at, 128:256] = got[96:192]
            return carry

        lax.fori_loop(0, NDP // GRP, unmix, 0)

    def give(kind, value):
        def mix(b, carry):
            at = pl.ds(pl.multiple_of(b * 96, 96), 96)
            v = value[at, :].astype(BF16)
            block = jnp.concatenate([v[:, 0:128], v[:, 128:256]], axis=0)
            got = mm(join, block, 1, 0).astype(BF16)
            bsend[kind, pl.ds(b * GRP, GRP)] = got.reshape(GRP, 3, 8, 128)
            return carry

        lax.fori_loop(0, NDP // GRP, mix, 0)

    def back(kind):
        def send(i, carry):
            d = partner(i, x, z, c)
            pltpu.make_async_remote_copy(
                src_ref=bsend.at[kind, d], dst_ref=brecv.at[kind, dp], send_sem=bsem_s, recv_sem=bsem_r.at[kind],
                device_id=(d, y), device_id_type=MESH,
            ).start()
            return carry

        lax.fori_loop(1, NDP, send, 0)
        pltpu.make_async_copy(bsend.at[kind, dp], brecv.at[kind, dp], bsem_r.at[kind]).start()

    take(0)
    for g in range(2):
        take(1 + g)
        if g == 1:
            back(0)

        def attend(b, carry):
            at = pl.ds(pl.multiple_of(b * HD, HD), HD)
            key, val = xs[0], xs[1]
            qb, gb = xs[2 + 2 * g, at, :], xs[3 + 2 * g, at, :]
            s = mm(key, qb, 1, 1) * SCALE
            ok = labk[:, 0:1] == rowv[0:1, at]
            s = jnp.where(ok, s, MASKED)
            top = jnp.max(s, axis=0, keepdims=True)
            e = jnp.exp(s - top)
            p = e * (1.0 / jnp.sum(e, axis=0, keepdims=True))
            d = mm(val, gb, 1, 1) - rowv[1 + g : 2 + g, at]
            ds = (p * d).astype(BF16)
            pv = mm(p.astype(BF16), gb, 1, 0)
            pk = mm(ds, qb, 1, 0)
            if g == 0:
                first = b == 0
                dv_acc[...] = jnp.where(first, 0.0, dv_acc[...]) + pv
                dk_acc[...] = jnp.where(first, 0.0, dk_acc[...]) + pk
            else:
                dv_acc[...] += pv
                dk_acc[...] += pk
            dq_acc[at, :] = mm(ds, key, 0, 0) * SCALE
            return carry

        if g == 0:
            dv_acc[...] = jnp.zeros((ROWS, HD), F32)
            dk_acc[...] = jnp.zeros((ROWS, HD), F32)
        lax.fori_loop(0, ROWS // HD, attend, 0)
        give(g, dq_acc)
    back(1)
    dk_acc[...] = dk_acc[...] * SCALE
    give(2, dk_acc)
    back(2)
    give(3, dv_acc)
    back(3)

    for kind in range(NB):
        pltpu.make_async_copy(brecv.at[kind], brecv.at[kind], bsem_r.at[kind]).wait()
        got = mm(gather[...], brecv[kind].reshape(2 * ROWS, 128), 1, 0).astype(BF16)
        for t in range(NY):
            obuf[kind, t, :, 0:128] = got[t * TOK : (t + 1) * TOK]
            obuf[kind, t, :, 128:256] = got[(NY + t) * TOK : (NY + t + 1) * TOK]
        ref = (oq_ref, oq_ref, ok_ref, ov_ref)[kind]
        if kind < 2:
            cols = pl.ds(pl.multiple_of(y * 2 * HD + kind * HD, HD), HD)
        else:
            cols = pl.ds(pl.multiple_of(y * HD, HD), HD)
        for dy in range(1, NY):
            t = lax.rem(y + dy, NY)
            pltpu.make_async_remote_copy(
                src_ref=obuf.at[kind, t], dst_ref=ref.at[:, cols], send_sem=osem_s, recv_sem=osem_r.at[max(0, kind - 1)],
                device_id=(dp, t), device_id_type=MESH,
            ).start()
        pltpu.make_async_copy(obuf.at[kind, y], ref.at[:, cols], osem_r.at[max(0, kind - 1)]).start()

    pltpu.make_async_copy(oq_ref, oq_ref, osem_r.at[0]).wait()
    pltpu.make_async_copy(ok_ref, ok_ref, osem_r.at[1]).wait()
    pltpu.make_async_copy(ov_ref, ov_ref, osem_r.at[2]).wait()
    some = pl.ds(0, NY - 1)
    pltpu.make_async_copy(meta_s.at[some], meta_s.at[some], ymsend).wait()
    pltpu.make_async_copy(tok.at[:, some], tok.at[:, some], ysend).wait()
    pltpu.make_async_copy(obuf.at[:, some], obuf.at[:, some], osem_s).wait()
    most = pl.ds(0, NDP - 1)
    pltpu.make_async_copy(msend.at[most], msend.at[most], zmsend).wait()
    pltpu.make_async_copy(fsend.at[:, most], fsend.at[:, most], zsend).wait()
    pltpu.make_async_copy(bsend.at[:, most], bsend.at[:, most], bsem_s).wait()


def body(queries, key_rows, values, saved_out, out_grad, pack_of, segment_label):
    anywhere = pl.BlockSpec(memory_space=pl.ANY)
    vmem = pl.BlockSpec(memory_space=pltpu.VMEM)
    dma = pltpu.SemaphoreType.DMA
    return pl.pallas_call(
        kernel,
        out_shape=(
            jax.ShapeDtypeStruct((TOK, 8 * HD), BF16),
            jax.ShapeDtypeStruct((TOK, 4 * HD), BF16),
            jax.ShapeDtypeStruct((TOK, 4 * HD), BF16),
        ),
        in_specs=[anywhere] * 3 + [vmem] * 5,
        out_specs=(anywhere,) * 3,
        scratch_shapes=[
            pltpu.VMEM((NT, NY, TOK, HD), BF16),
            pltpu.VMEM((NY, 8, TOK), F32),
            pltpu.VMEM((NY, 8, TOK), F32),
            pltpu.VMEM((2 * ROWS, 2 * NY * TOK), BF16),
            pltpu.VMEM((2 * NY * TOK, 2 * ROWS), BF16),
            pltpu.VMEM((3, NDP, 6, 8, 128), BF16),
            pltpu.VMEM((3, NDP, 6, 8, 128), BF16),
            pltpu.VMEM((NDP, 1, 128), F32),
            pltpu.VMEM((NDP, 1, 128), F32),
            pltpu.VMEM((NT, ROWS, HD), BF16),
            pltpu.VMEM((8, ROWS), F32),
            pltpu.VMEM((ROWS, 128), F32),
            pltpu.VMEM((ROWS, HD), F32),
            pltpu.VMEM((ROWS, HD), F32),
            pltpu.VMEM((ROWS, HD), F32),
            pltpu.VMEM((NB, NDP, 3, 8, 128), BF16),
            pltpu.VMEM((NB, NDP, 3, 8, 128), BF16),
            pltpu.VMEM((NB, NY, TOK, HD), BF16),
            dma, dma((3,)), dma, dma, dma, dma((3,)), dma, dma, dma, dma((NB,)), dma, dma((3,)),
        ],
        compiler_params=pltpu.CompilerParams(
            collective_id=0, has_side_effects=True, vmem_limit_bytes=52 << 20
        ),
        name="packed_attention_backward",
    )(
        queries, key_rows, values, out_grad, saved_out,
        pack_of, pack_of.reshape(1, TOK), segment_label.reshape(1, TOK),
    )


def solution(mesh):
    rows = P(("dp", "ctx"), None)
    return jax.shard_map(
        body,
        mesh=mesh,
        in_specs=(rows, rows, rows, rows, rows, rows, P(("dp", "ctx"))),
        out_specs=(rows, rows, rows),
        check_vma=False,
    )
```

time: 292 us -> 133 us (0.46)
  waiting for transfers between devices: 135 us -> 0 us
  Pallas kernels: 0 us -> 127 us
  starting transfers between devices: 64.6 us -> 0 us
  local copies, waits for them, and re-layouts: 41.8 us -> 5.4 us
  matrix products: 14.8 us -> 0 us
  between operations: 15 us -> 0.65 us
  other arithmetic: 9.79 us -> 0 us
  blocking collectives: 9.29 us -> 0 us
    all_to_all x9 -> x0, waiting for transfers between devices: 133 us -> none  [the longest x1 25.4 us: body(): lax.all_to_all(grad_q, 'dp', split_axis=0, concat_axis=0, tiled=True)]
    pallas_call x0 -> x1, Pallas kernels: none -> 127 us  [body(): pl.pallas_call(kernel, out_shape=(jax.ShapeDtypeStruct((TOK, 8 * HD), BF1...]
    all_to_all x9 -> x0, starting transfers between devices: 64.2 us -> none  [the longest x1 13 us: body(): lax.all_to_all(labels, 'dp', split_axis=0, concat_axis=0, tiled=True)]
    all_to_all x16 -> x0, local copies, waits for them, and re-layouts: 15.2 us -> none  [the longest x2 2.4 us: body(): lax.all_to_all(grad_k, 'dp', split_axis=0, concat_axis=0, tiled=True)]
    dot_general x20 -> x0, matrix products: 14.8 us -> none  [the longest x4 5.39 us: body(): jnp.einsum('grk,kd->rgd', dscore, key_head, preferred_element_type=jnp.fl...]
    unnamed x1 -> x0, blocking collectives: 9.29 us -> none
    scatter x5 -> x0, local copies, waits for them, and re-layouts: 8.9 us -> none  [to_slots(): jnp.zeros((slots,) + matrix.shape[1:], matrix.dtype).at[position]]
    gather x3 -> x0, local copies, waits for them, and re-layouts: 4.85 us -> none  [body(): return (back_q[position], back_k[position], back_v[position])]
  transfers between devices with their start and end apart: 13 -> 0, of which waited for: 11 -> 0; matrix products, arithmetic and copies ran while one was open for 11% -> 0% of each run, Pallas kernels for 0% -> 0%
where the time goes in v1:
time: 133 us
  Pallas kernels  127 us (95%)
  local copies, waits for them, and re-layouts  5.4 us (4%)
    pallas_call x1, Pallas kernels, body(): pl.pallas_call(kernel, out_shape=(jax.ShapeDtypeStruct((TOK, 8 * HD), BF1...  127 us
    unnamed x12, local copies, waits for them, and re-layouts  5.4 us

profile of v1, /device:TPU:1, one launch (start us, length us, event | category | flops | bytes accessed | tf_op | source)
XLA Modules:
  0.0 132.6 jit_solution(7025587508088903095)
XLA Ops:
  0.6 0.0 copy-start.2
  0.6 0.6 copy-done.2
  1.3 0.0 copy-start.3
  1.3 0.1 copy.10.pcol_ref
  1.4 0.5 copy-done.3
  1.9 0.0 copy-start
  1.9 0.9 copy-done
  2.9 0.0 copy-start.1
  2.9 0.9 copy-done.1
  3.8 126.6 %packed_attention_backward.1 = (bf16[128,2048]{1,0:T(8,128)(2,1)S(1)}, bf16[128,1024]{1,0:T(8,128)(2,1)S(1)}, bf16[128,1024]{1,0:T(8,128)(2,1)S(1)}) custom-call(bf16[128,2048]{1,0:T(8,128)(2,1)} %q_ref.1, bf16[128,1024]{1,0:T(8,128)(2,1)S(1)} %copy-done, bf16[128,1024]{1,0:T(8,128)(2,1)S(1)} %copy-done.1, bf16[128,2048]{1,0:T(8,128)(2,1)} %g_ref.1, ...), custom_call_target="tpu_custom_call" | custom-call | tf_op jit(solution)/shard_map/packed_attention_backward/pallas_call | solution.py:309
  130.4 0.8 copy.14
  131.2 0.7 copy.15
  131.9 0.7 copy.16
Async XLA Ops:
  0.6 0.7 copy-start.2
  1.3 0.7 copy-start.3
  1.9 0.9 copy-start
  2.9 0.9 copy-start.1

commit v2 on v1

v2 whole, which is shorter than its diff:
```python
import jax
import jax.numpy as jnp
from jax import lax
from jax.experimental import pallas as pl
from jax.experimental.pallas import tpu as pltpu
from jax.sharding import PartitionSpec as P

MESH = pl.DeviceIdType.MESH
F32 = jnp.float32
BF16 = jnp.bfloat16

NDP = 64
NY = 4
TOK = 128
CAP = 3
HD = 256
SLOT = NY * CAP
ROWS = NDP * SLOT
GRP = 8
MASKED = -1e30
SCALE = 1.0 / 16.0

NT, NB = 6, 4


def iota(shape, dim):
    return lax.broadcasted_iota(jnp.int32, shape, dim)


def mm(a, b, ca, cb):
    return lax.dot_general(a, b, (((ca,), (cb,)), ((), ())), preferred_element_type=F32)


def kernel(
    q_ref, k_ref, v_ref, g_ref, o_ref, pack_ref, lab_ref,
    oq_ref, ok_ref, ov_ref,
    ints, gv, ov, tok, meta_s, meta_r, del_s, del_r, place, gather, fsend, frecv, msend, mrecv, xs, rowv, labk,
    dq_acc, dk_acc, dv_acc, bsend, brecv, obuf,
    insem, isem, ysend, yrecv, ymsend, ymrecv, ydsend, ydrecv, zsend, zrecv, zmsend, zmrecv,
    bsem_s, bsem_r, osem_s, osem_r, plane_sem, core_sem,
):
    dp = lax.axis_index("dp")
    y = lax.axis_index("ctx")
    x, z, c = dp // 16, lax.rem(dp // 2, 8), lax.rem(dp, 2)
    bar = pltpu.get_barrier_semaphore()

    def at(nx, nz, nc):
        return (nx * 8 + nz) * 2 + nc

    def greet(sem, d, t):
        pl.semaphore_signal(sem, inc=1, device_id=(d, t), device_id_type=MESH)

    ring_x = [at(lax.rem(x + j, 4), z, c) for j in range(1, 4)]
    other = at(x, z, 1 - c)
    ring_y = [lax.rem(y + j, NY) for j in range(1, NY)]
    for t in ring_y:
        greet(bar, dp, t)
    for d in ring_x:
        greet(bar, d, y)
    greet(bar, other, y)
    for j in range(1, 8):
        greet(bar, at(x, lax.rem(z + j, 8), c), y)

    copies = [
        pltpu.make_async_copy(pack_ref, ints.at[0], isem.at[0]),
        pltpu.make_async_copy(lab_ref, ints.at[1], isem.at[1]),
        pltpu.make_async_copy(g_ref, gv, insem.at[0]),
        pltpu.make_async_copy(o_ref, ov, insem.at[1]),
    ]
    for copy in copies:
        copy.start()

    def columns(kind, head):
        if kind == 0:
            return k_ref.at[:, pl.ds(pl.multiple_of(head * HD, HD), HD)]
        if kind == 1:
            return v_ref.at[:, pl.ds(pl.multiple_of(head * HD, HD), HD)]
        ref = q_ref if kind % 2 == 0 else g_ref
        return ref.at[:, pl.ds(pl.multiple_of(head * 2 * HD + (kind // 2 - 1) * HD, HD), HD)]

    for kind in range(NT):
        pltpu.make_async_copy(columns(kind, y), tok.at[kind, y], yrecv.at[kind]).start()

    eye = (iota((TOK, TOK), 0) == iota((TOK, TOK), 1)).astype(F32).astype(BF16)
    copies[0].wait()
    copies[1].wait()
    prow = ints[0].astype(F32)
    pcol = mm(eye, jnp.broadcast_to(prow, (8, TOK)).astype(BF16), 1, 1)[:, 0:1]
    earlier = (pcol == prow) & (iota((TOK, TOK), 0) < iota((TOK, TOK), 1))
    rank = jnp.sum(earlier.astype(F32), axis=0, keepdims=True)
    slot = rank + (y * CAP).astype(F32)
    meta_s[0:1, :] = prow
    meta_s[1:2, :] = slot
    meta_s[2:3, :] = ints[1].astype(F32) + 1.0
    meta_s[3:8, :] = jnp.zeros((5, TOK), F32)
    meta_r[y] = meta_s[...]

    pl.semaphore_wait(bar, 14)

    for t in ring_y:
        pltpu.make_async_remote_copy(
            src_ref=meta_s, dst_ref=meta_r.at[y], send_sem=ymsend, recv_sem=ymrecv,
            device_id=(dp, t), device_id_type=MESH,
        ).start()
    for kind in range(NT):
        for t in ring_y:
            pltpu.make_async_remote_copy(
                src_ref=columns(kind, t), dst_ref=tok.at[kind, y], send_sem=ysend, recv_sem=yrecv.at[kind],
                device_id=(dp, t), device_id_type=MESH,
            ).start()

    for d in ring_x:
        greet(plane_sem, d, y)
    pl.semaphore_wait(plane_sem, 3)
    greet(core_sem, other, y)
    pl.semaphore_wait(core_sem, 1)

    pltpu.make_async_copy(meta_r.at[pl.ds(0, NY - 1)], meta_r.at[pl.ds(0, NY - 1)], ymrecv).wait()
    packs = jnp.concatenate([meta_r[t, 0:1, :] for t in range(NY)], axis=1)
    slots = jnp.concatenate([meta_r[t, 1:2, :] for t in range(NY)], axis=1)
    where = (packs * (2.0 * SLOT) + slots).astype(jnp.int32)

    def place_block(b, carry):
        r = iota((HD, NY * TOK), 0) + b * HD
        at = pl.ds(pl.multiple_of(b * HD, HD), HD)
        place[at, 0 : NY * TOK] = (r == where).astype(F32).astype(BF16)
        place[at, NY * TOK : 2 * NY * TOK] = (r == where + SLOT).astype(F32).astype(BF16)
        return carry

    lax.fori_loop(0, 2 * ROWS // HD, place_block, 0)

    base = dp // GRP
    spin = [lax.rem(dp + j, GRP) for j in range(GRP)]

    def spread_out(g, src, dst, ssem, rsem):
        for j in range(GRP):
            d = g * GRP + spin[j]

            @pl.when(d != dp)
            def _():
                pltpu.make_async_remote_copy(
                    src_ref=src.at[d], dst_ref=dst.at[dp], send_sem=ssem, recv_sem=rsem,
                    device_id=(d, y), device_id_type=MESH,
                ).start()

    def forward(kind):
        pltpu.make_async_copy(tok.at[kind], tok.at[kind], yrecv.at[kind]).wait()

        def fill(k, carry):
            g = lax.rem(base + k, GRP)
            t = tok[kind].reshape(NY * TOK, HD)
            halves = jnp.concatenate([t[:, 0:128], t[:, 128:256]], axis=0)
            got = mm(place[pl.ds(pl.multiple_of(g * 192, 192), 192), :], halves, 1, 0)
            fsend[kind, pl.ds(g * GRP, GRP)] = got.astype(BF16).reshape(GRP, 3, 8, 128)
            spread_out(g, fsend.at[kind], frecv.at[kind], zsend, zrecv.at[kind])
            return carry

        lax.fori_loop(1, GRP + 1, fill, 0)
        pltpu.make_async_copy(fsend.at[kind, dp], frecv.at[kind, dp], zrecv.at[kind]).start()

    for kind in range(NT):
        forward(kind)
        if kind == 0:
            copies[2].wait()
            copies[3].wait()
            prod = gv[...].astype(F32) * ov[...].astype(F32)
            hi = prod.astype(BF16)
            lo = (prod - hi.astype(F32)).astype(BF16)
            pick = (iota((8, 8 * HD), 1) // HD == iota((8, 8 * HD), 0)).astype(BF16)
            delta = (mm(pick, hi, 1, 1) + mm(pick, lo, 1, 1)).astype(BF16).astype(F32)
            for t in range(NY):
                del_s[t, 0:2, :] = delta[2 * t : 2 * t + 2, :]
                del_s[t, 2:8, :] = jnp.zeros((6, TOK), F32)
            del_r[y] = del_s[y]
            for t in ring_y:
                pltpu.make_async_remote_copy(
                    src_ref=del_s.at[t], dst_ref=del_r.at[y], send_sem=ydsend, recv_sem=ydrecv,
                    device_id=(dp, t), device_id_type=MESH,
                ).start()
        if kind == 1:
            pltpu.make_async_copy(del_r.at[pl.ds(0, NY - 1)], del_r.at[pl.ds(0, NY - 1)], ydrecv).wait()
            owner = (iota((NDP, NY * TOK), 0).astype(F32) == packs).astype(F32).astype(BF16)
            lane = iota((128, NY * TOK), 0)
            vals = [jnp.concatenate([meta_r[t, 2:3, :] for t in range(NY)], axis=1)]
            vals += [jnp.concatenate([del_r[t, j : j + 1, :] for t in range(NY)], axis=1) for j in range(2)]
            kindv = jnp.where(lane // 16 == 0, vals[0], jnp.where(lane // 16 == 1, vals[1], vals[2]))
            hit = (lax.rem(lane, 16).astype(F32) == slots) & (lane < 48)
            small = jnp.where(hit, kindv, 0.0).astype(BF16)
            msend[...] = mm(owner, small, 1, 1).reshape(NDP, 1, 128)

            def meta_out(k, carry):
                spread_out(lax.rem(base + k, GRP), msend, mrecv, zmsend, zmrecv)
                return carry

            lax.fori_loop(1, GRP + 1, meta_out, 0)
            pltpu.make_async_copy(msend.at[dp], mrecv.at[dp], zmrecv).start()

    for t in range(NY):
        col = mm(eye, meta_r[t].astype(BF16), 1, 1)
        home = (col[:, 0:1] * (2.0 * SLOT) + col[:, 1:2]).astype(jnp.int32)
        for half in range(2):
            row = half * NY * TOK + t * TOK

            def gather_block(b, carry):
                r = iota((TOK, HD), 1) + b * HD
                gather[row : row + TOK, pl.ds(pl.multiple_of(b * HD, HD), HD)] = (
                    (r == home + half * SLOT).astype(F32).astype(BF16)
                )
                return carry

            lax.fori_loop(0, 2 * ROWS // HD, gather_block, 0)

    a, b = iota((192, 192), 0), iota((192, 192), 1)
    split = (b == (lax.rem(a, 96) // 12) * 24 + (a // 96) * 12 + lax.rem(a, 12)).astype(F32).astype(BF16)
    join = (a == (lax.rem(b, 96) // 12) * 24 + (b // 96) * 12 + lax.rem(b, 12)).astype(F32).astype(BF16)

    pltpu.make_async_copy(mrecv, mrecv, zmrecv).wait()
    spread = (iota((ROWS, NDP), 0) // SLOT == iota((ROWS, NDP), 1)).astype(F32).astype(BF16)
    rows = mm(spread, mrecv[...].reshape(NDP, 128).astype(BF16), 1, 0)
    r12, l128 = lax.rem(iota((ROWS, 128), 0), SLOT), iota((ROWS, 128), 1)
    own = jnp.where((lax.rem(l128, 16) == r12) & (l128 < 48), rows, 0.0)
    labcol = jnp.sum(jnp.where(l128 < 16, own, 0.0), axis=1, keepdims=True)
    labk[...] = jnp.broadcast_to(jnp.where(labcol > 0.5, labcol, -1.0), (ROWS, 128))
    pick16 = (iota((8, 128), 1) // 16 == iota((8, 128), 0)).astype(F32).astype(BF16)
    rowv[...] = mm(pick16, own.astype(BF16), 1, 1)

    def arrive(kind):
        pltpu.make_async_copy(frecv.at[kind], frecv.at[kind], zrecv.at[kind]).wait()

    def take(kind):
        def unmix(b, carry):
            block = frecv[kind, pl.ds(b * GRP, GRP)].reshape(192, 128)
            got = mm(split, block, 1, 0).astype(BF16)
            at = pl.ds(pl.multiple_of(b * 96, 96), 96)
            xs[kind, at, 0:128] = got[0:96]
            xs[kind, at, 128:256] = got[96:192]
            return carry

        lax.fori_loop(0, NDP // GRP, unmix, 0)

    def give(kind, value):
        def mix(b, carry):
            at = pl.ds(pl.multiple_of(b * 96, 96), 96)
            v = value[at, :].astype(BF16)
            block = jnp.concatenate([v[:, 0:128], v[:, 128:256]], axis=0)
            got = mm(join, block, 1, 0).astype(BF16)
            bsend[kind, pl.ds(b * GRP, GRP)] = got.reshape(GRP, 3, 8, 128)
            return carry

        lax.fori_loop(0, NDP // GRP, mix, 0)

    def back(kind):
        def send(k, carry):
            spread_out(lax.rem(base + k, GRP), bsend.at[kind], brecv.at[kind], bsem_s, bsem_r.at[kind])
            return carry

        lax.fori_loop(1, GRP + 1, send, 0)
        pltpu.make_async_copy(bsend.at[kind, dp], brecv.at[kind, dp], bsem_r.at[kind]).start()

    for kind in range(2):
        arrive(kind)
        take(kind)
    for g in range(2):
        arrive(2 + 2 * g)
        take(2 + 2 * g)
        arrive(3 + 2 * g)
        if g == 1:
            back(0)
        take(3 + 2 * g)

        def attend(b, carry):
            at = pl.ds(pl.multiple_of(b * HD, HD), HD)
            key, val = xs[0], xs[1]
            qb, gb = xs[2 + 2 * g, at, :], xs[3 + 2 * g, at, :]
            s = mm(key, qb, 1, 1) * SCALE
            ok = labk[:, 0:1] == rowv[0:1, at]
            s = jnp.where(ok, s, MASKED)
            top = jnp.max(s, axis=0, keepdims=True)
            e = jnp.exp(s - top)
            p = e * (1.0 / jnp.sum(e, axis=0, keepdims=True))
            d = mm(val, gb, 1, 1) - rowv[1 + g : 2 + g, at]
            ds = (p * d).astype(BF16)
            pv = mm(p.astype(BF16), gb, 1, 0)
            pk = mm(ds, qb, 1, 0)
            if g == 0:
                first = b == 0
                dv_acc[...] = jnp.where(first, 0.0, dv_acc[...]) + pv
                dk_acc[...] = jnp.where(first, 0.0, dk_acc[...]) + pk
            else:
                dv_acc[...] += pv
                dk_acc[...] += pk
            dq_acc[at, :] = mm(ds, key, 0, 0) * SCALE
            return carry

        if g == 0:
            dv_acc[...] = jnp.zeros((ROWS, HD), F32)
            dk_acc[...] = jnp.zeros((ROWS, HD), F32)
        lax.fori_loop(0, ROWS // HD, attend, 0)
        give(g, dq_acc)
    back(1)
    dk_acc[...] = dk_acc[...] * SCALE
    give(2, dk_acc)
    back(2)
    give(3, dv_acc)
    back(3)

    for kind in range(NB):
        pltpu.make_async_copy(brecv.at[kind], brecv.at[kind], bsem_r.at[kind]).wait()
        got = mm(gather[...], brecv[kind].reshape(2 * ROWS, 128), 1, 0).astype(BF16)
        for t in range(NY):
            obuf[kind, t, :, 0:128] = got[t * TOK : (t + 1) * TOK]
            obuf[kind, t, :, 128:256] = got[(NY + t) * TOK : (NY + t + 1) * TOK]
        ref = (oq_ref, oq_ref, ok_ref, ov_ref)[kind]
        if kind < 2:
            cols = pl.ds(pl.multiple_of(y * 2 * HD + kind * HD, HD), HD)
        else:
            cols = pl.ds(pl.multiple_of(y * HD, HD), HD)
        for t in ring_y:
            pltpu.make_async_remote_copy(
                src_ref=obuf.at[kind, t], dst_ref=ref.at[:, cols], send_sem=osem_s, recv_sem=osem_r.at[max(0, kind - 1)],
                device_id=(dp, t), device_id_type=MESH,
            ).start()
        pltpu.make_async_copy(obuf.at[kind, y], ref.at[:, cols], osem_r.at[max(0, kind - 1)]).start()

    pltpu.make_async_copy(oq_ref, oq_ref, osem_r.at[0]).wait()
    pltpu.make_async_copy(ok_ref, ok_ref, osem_r.at[1]).wait()
    pltpu.make_async_copy(ov_ref, ov_ref, osem_r.at[2]).wait()
    some = pl.ds(0, NY - 1)
    pltpu.make_async_copy(meta_r.at[some], meta_r.at[some], ymsend).wait()
    pltpu.make_async_copy(del_r.at[some], del_r.at[some], ydsend).wait()
    pltpu.make_async_copy(tok.at[:, some], tok.at[:, some], ysend).wait()
    pltpu.make_async_copy(obuf.at[:, some], obuf.at[:, some], osem_s).wait()
    most = pl.ds(0, NDP - 1)
    pltpu.make_async_copy(msend.at[most], msend.at[most], zmsend).wait()
    pltpu.make_async_copy(fsend.at[:, most], fsend.at[:, most], zsend).wait()
    pltpu.make_async_copy(bsend.at[:, most], bsend.at[:, most], bsem_s).wait()


def body(queries, key_rows, values, saved_out, out_grad, pack_of, segment_label):
    anywhere = pl.BlockSpec(memory_space=pl.ANY)
    hbm = pl.BlockSpec(memory_space=pltpu.HBM)
    dma = pltpu.SemaphoreType.DMA
    return pl.pallas_call(
        kernel,
        out_shape=(
            jax.ShapeDtypeStruct((TOK, 8 * HD), BF16),
            jax.ShapeDtypeStruct((TOK, 4 * HD), BF16),
            jax.ShapeDtypeStruct((TOK, 4 * HD), BF16),
        ),
        in_specs=[hbm] * 7,
        out_specs=(anywhere,) * 3,
        scratch_shapes=[
            pltpu.VMEM((2, 1, TOK), jnp.int32),
            pltpu.VMEM((TOK, 8 * HD), BF16),
            pltpu.VMEM((TOK, 8 * HD), BF16),
            pltpu.VMEM((NT, NY, TOK, HD), BF16),
            pltpu.VMEM((8, TOK), F32),
            pltpu.VMEM((NY, 8, TOK), F32),
            pltpu.VMEM((NY, 8, TOK), F32),
            pltpu.VMEM((NY, 8, TOK), F32),
            pltpu.VMEM((2 * ROWS, 2 * NY * TOK), BF16),
            pltpu.VMEM((2 * NY * TOK, 2 * ROWS), BF16),
            pltpu.VMEM((NT, NDP, 3, 8, 128), BF16),
            pltpu.VMEM((NT, NDP, 3, 8, 128), BF16),
            pltpu.VMEM((NDP, 1, 128), F32),
            pltpu.VMEM((NDP, 1, 128), F32),
            pltpu.VMEM((NT, ROWS, HD), BF16),
            pltpu.VMEM((8, ROWS), F32),
            pltpu.VMEM((ROWS, 128), F32),
            pltpu.VMEM((ROWS, HD), F32),
            pltpu.VMEM((ROWS, HD), F32),
            pltpu.VMEM((ROWS, HD), F32),
            pltpu.VMEM((NB, NDP, 3, 8, 128), BF16),
            pltpu.VMEM((NB, NDP, 3, 8, 128), BF16),
            pltpu.VMEM((NB, NY, TOK, HD), BF16),
            dma((2,)), dma((2,)), dma, dma((NT,)), dma, dma, dma, dma, dma, dma((NT,)), dma, dma,
            dma, dma((NB,)), dma, dma((3,)),
            pltpu.SemaphoreType.REGULAR, pltpu.SemaphoreType.REGULAR,
        ],
        compiler_params=pltpu.CompilerParams(
            collective_id=0, has_side_effects=True, vmem_limit_bytes=52 << 20
        ),
        name="packed_attention_backward",
    )(
        queries, key_rows, values, out_grad, saved_out,
        pack_of.reshape(1, TOK), segment_label.reshape(1, TOK),
    )


def solution(mesh):
    rows = P(("dp", "ctx"), None)
    return jax.shard_map(
        body,
        mesh=mesh,
        in_specs=(rows, rows, rows, rows, rows, rows, P(("dp", "ctx"))),
        out_specs=(rows, rows, rows),
        check_vma=False,
    )
```

time: 133 us -> 118 us (0.89)
  Pallas kernels: 127 us -> 112 us
    pallas_call x1, Pallas kernels: 127 us -> 112 us  [body(): pl.pallas_call(kernel, out_shape=(jax.ShapeDtypeStruct((TOK, 8 * HD), BF1...]
    unnamed x12 -> x11, local copies, waits for them, and re-layouts: 5.4 us -> 4.75 us
where the time goes in v2:
time: 118 us
  Pallas kernels  112 us (95%)
  local copies, waits for them, and re-layouts  4.75 us (4%)
    pallas_call x1, Pallas kernels, body(): pl.pallas_call(kernel, out_shape=(jax.ShapeDtypeStruct((TOK, 8 * HD), BF1...  112 us
    unnamed x11, local copies, waits for them, and re-layouts  4.75 us

profile of v2, /device:TPU:1, one launch (start us, length us, event | category | flops | bytes accessed | tf_op | source)
XLA Modules:
  0.0 117.5 jit_solution(15304538671063290633)
XLA Ops:
  0.6 0.0 copy-start.2
  0.6 0.0 copy-start.3
  0.7 0.6 copy-done.2
  1.3 0.0 copy-done.3
  1.3 0.0 copy-start
  1.3 0.9 copy-done
  2.3 0.0 copy-start.1
  2.3 0.9 copy-done.1
  3.2 112.1 %packed_attention_backward.1 = (bf16[128,2048]{1,0:T(8,128)(2,1)S(1)}, bf16[128,1024]{1,0:T(8,128)(2,1)S(1)}, bf16[128,1024]{1,0:T(8,128)(2,1)S(1)}) custom-call(bf16[128,2048]{1,0:T(8,128)(2,1)} %q_ref.1, bf16[128,1024]{1,0:T(8,128)(2,1)S(1)} %copy-done, bf16[128,1024]{1,0:T(8,128)(2,1)S(1)} %copy-done.1, bf16[128,2048]{1,0:T(8,128)(2,1)} %g_ref.1, ...), custom_call_target="tpu_custom_call" | custom-call | tf_op jit(solution)/shard_map/packed_attention_backward/pallas_call | solution.py:343
  115.3 0.8 copy.13
  116.1 0.7 copy.14
  116.8 0.7 copy.15
Async XLA Ops:
  0.6 0.7 copy-start.2
  0.6 0.7 copy-start.3
  1.3 0.9 copy-start
  2.3 0.9 copy-start.1

commit v3 on v2

--- a/solution.py
+++ b/solution.py
@@ -17,6 +17,7 @@
 SLOT = NY * CAP
 ROWS = NDP * SLOT
 GRP = 8
+PLANE = 16
 MASKED = -1e30
 SCALE = 1.0 / 16.0
 
@@ -35,8 +36,9 @@
     q_ref, k_ref, v_ref, g_ref, o_ref, pack_ref, lab_ref,
     oq_ref, ok_ref, ov_ref,
     ints, gv, ov, tok, meta_s, meta_r, del_s, del_r, place, gather, fsend, frecv, msend, mrecv, xs, rowv, labk,
-    dq_acc, dk_acc, dv_acc, bsend, brecv, obuf,
-    insem, isem, ysend, yrecv, ymsend, ymrecv, ydsend, ydrecv, zsend, zrecv, zmsend, zmrecv,
+    dq_acc, dk_acc, dv_acc, bsend, brecv, obuf, fsend2, frecv2, bsend2, brecv2,
+    kv, kplace, kgather, ksend, krecv, dksend, dkrecv,
+    ksem, kysend, kyrecv, insem, isem, ysend, yrecv, ymsend, ymrecv, ydsend, ydrecv, zsend, zrecv, zmsend, zmrecv,
     bsem_s, bsem_r, osem_s, osem_r, plane_sem, core_sem,
 ):
     dp = lax.axis_index("dp")
@@ -66,19 +68,18 @@
         pltpu.make_async_copy(lab_ref, ints.at[1], isem.at[1]),
         pltpu.make_async_copy(g_ref, gv, insem.at[0]),
         pltpu.make_async_copy(o_ref, ov, insem.at[1]),
+        pltpu.make_async_copy(k_ref, kv, ksem),
     ]
-    for copy in copies:
-        copy.start()
+    for n in (0, 1, 4, 2, 3):
+        copies[n].start()
 
     def columns(kind, head):
-        if kind == 0:
-            return k_ref.at[:, pl.ds(pl.multiple_of(head * HD, HD), HD)]
         if kind == 1:
             return v_ref.at[:, pl.ds(pl.multiple_of(head * HD, HD), HD)]
         ref = q_ref if kind % 2 == 0 else g_ref
         return ref.at[:, pl.ds(pl.multiple_of(head * 2 * HD + (kind // 2 - 1) * HD, HD), HD)]
 
-    for kind in range(NT):
+    for kind in range(1, NT):
         pltpu.make_async_copy(columns(kind, y), tok.at[kind, y], yrecv.at[kind]).start()
 
     eye = (iota((TOK, TOK), 0) == iota((TOK, TOK), 1)).astype(F32).astype(BF16)
@@ -102,7 +103,7 @@
             src_ref=meta_s, dst_ref=meta_r.at[y], send_sem=ymsend, recv_sem=ymrecv,
             device_id=(dp, t), device_id_type=MESH,
         ).start()
-    for kind in range(NT):
+    for kind in range(1, NT):
         for t in ring_y:
             pltpu.make_async_remote_copy(
                 src_ref=columns(kind, t), dst_ref=tok.at[kind, y], send_sem=ysend, recv_sem=yrecv.at[kind],
@@ -115,6 +116,48 @@
     greet(core_sem, other, y)
     pl.semaphore_wait(core_sem, 1)
 
+    own_row = (prow * (2.0 * SLOT) + rank).astype(jnp.int32)
+
+    def kplace_block(b, carry):
+        r = iota((HD, TOK), 0) + b * HD
+        at = pl.ds(pl.multiple_of(b * HD, HD), HD)
+        for cb in range(8):
+            kplace[at, cb * TOK : (cb + 1) * TOK] = (r == own_row + CAP * cb).astype(F32).astype(BF16)
+        return carry
+
+    lax.fori_loop(0, 2 * ROWS // HD, kplace_block, 0)
+
+    spin = [lax.rem(dp + j, PLANE) for j in range(PLANE)]
+
+    def plane(k):
+        return lax.rem(x + k, 4)
+
+    def spread_out(g, first, src, dst, ssem, rsem):
+        for j in range(first, PLANE):
+            d = g * PLANE + spin[j]
+            pltpu.make_async_remote_copy(
+                src_ref=src.at[d], dst_ref=dst.at[dp], send_sem=ssem, recv_sem=rsem,
+                device_id=(d, y), device_id_type=MESH,
+            ).start()
+
+    copies[4].wait()
+
+    def fill_k(g):
+        at = pl.ds(pl.multiple_of(g * 24 * PLANE, 24 * PLANE), 24 * PLANE)
+        stack = jnp.concatenate([kv[:, cb * TOK : (cb + 1) * TOK] for cb in range(8)], axis=0)
+        got = mm(kplace[at, :], stack, 1, 0)
+        fsend[0, pl.ds(g * PLANE, PLANE)] = got.astype(BF16).reshape(PLANE, 3, 8, 128)
+
+    def step_k(k, carry):
+        fill_k(plane(k))
+        spread_out(plane(k), 0, fsend.at[0], frecv.at[0], zsend, zrecv.at[0])
+        return carry
+
+    lax.fori_loop(1, 4, step_k, 0)
+    fill_k(x)
+    spread_out(x, 1, fsend.at[0], frecv.at[0], zsend, zrecv.at[0])
+    pltpu.make_async_copy(fsend.at[0, dp], frecv.at[0, dp], zrecv.at[0]).start()
+
     pltpu.make_async_copy(meta_r.at[pl.ds(0, NY - 1)], meta_r.at[pl.ds(0, NY - 1)], ymrecv).wait()
     packs = jnp.concatenate([meta_r[t, 0:1, :] for t in range(NY)], axis=1)
     slots = jnp.concatenate([meta_r[t, 1:2, :] for t in range(NY)], axis=1)
@@ -129,37 +172,68 @@
 
     lax.fori_loop(0, 2 * ROWS // HD, place_block, 0)
 
-    base = dp // GRP
-    spin = [lax.rem(dp + j, GRP) for j in range(GRP)]
-
-    def spread_out(g, src, dst, ssem, rsem):
-        for j in range(GRP):
-            d = g * GRP + spin[j]
-
-            @pl.when(d != dp)
-            def _():
-                pltpu.make_async_remote_copy(
-                    src_ref=src.at[d], dst_ref=dst.at[dp], send_sem=ssem, recv_sem=rsem,
-                    device_id=(d, y), device_id_type=MESH,
-                ).start()
+    def everyone(src, dst, ssem, rsem):
+        def send(k, carry):
+            spread_out(plane(k), 0, src, dst, ssem, rsem)
+            return carry
+
+        lax.fori_loop(1, 4, send, 0)
+        spread_out(x, 1, src, dst, ssem, rsem)
+        pltpu.make_async_copy(src.at[dp], dst.at[dp], rsem).start()
+
+    def landed(kind):
+        pltpu.make_async_copy(tok.at[kind], tok.at[kind], yrecv.at[kind]).wait()
+
+    def weave(kind):
+        t = tok[kind].reshape(NY * TOK, HD)
+        return jnp.concatenate([t[:, 0:128], t[:, 128:256]], axis=0)
+
+    def placed(g):
+        return place[pl.ds(pl.multiple_of(g * 24 * PLANE, 24 * PLANE), 24 * PLANE), :]
 
     def forward(kind):
-        pltpu.make_async_copy(tok.at[kind], tok.at[kind], yrecv.at[kind]).wait()
-
-        def fill(k, carry):
-            g = lax.rem(base + k, GRP)
-            t = tok[kind].reshape(NY * TOK, HD)
-            halves = jnp.concatenate([t[:, 0:128], t[:, 128:256]], axis=0)
-            got = mm(place[pl.ds(pl.multiple_of(g * 192, 192), 192), :], halves, 1, 0)
-            fsend[kind, pl.ds(g * GRP, GRP)] = got.astype(BF16).reshape(GRP, 3, 8, 128)
-            spread_out(g, fsend.at[kind], frecv.at[kind], zsend, zrecv.at[kind])
-            return carry
-
-        lax.fori_loop(1, GRP + 1, fill, 0)
+        landed(kind)
+
+        def fill(g):
+            got = mm(placed(g), weave(kind), 1, 0)
+            fsend[kind, pl.ds(g * PLANE, PLANE)] = got.astype(BF16).reshape(PLANE, 3, 8, 128)
+
+        def step(k, carry):
+            fill(plane(k))
+            spread_out(plane(k), 0, fsend.at[kind], frecv.at[kind], zsend, zrecv.at[kind])
+            return carry
+
+        lax.fori_loop(1, 4, step, 0)
+        fill(x)
+        spread_out(x, 1, fsend.at[kind], frecv.at[kind], zsend, zrecv.at[kind])
         pltpu.make_async_copy(fsend.at[kind, dp], frecv.at[kind, dp], zrecv.at[kind]).start()
 
-    for kind in range(NT):
-        forward(kind)
+    def forward2(h):
+        landed(2 + 2 * h)
+        landed(3 + 2 * h)
+
+        def fill(g):
+            both = jnp.concatenate([weave(2 + 2 * h), weave(3 + 2 * h)], axis=1)
+            got = mm(placed(g), both, 1, 0).astype(BF16)
+            here = pl.ds(g * PLANE, PLANE)
+            fsend2[h, here, 0:3] = got[:, 0:128].reshape(PLANE, 3, 8, 128)
+            fsend2[h, here, 3:6] = got[:, 128:256].reshape(PLANE, 3, 8, 128)
+
+        def step(k, carry):
+            fill(plane(k))
+            spread_out(plane(k), 0, fsend2.at[h], frecv2.at[h], zsend, zrecv.at[2 + h])
+            return carry
+
+        lax.fori_loop(1, 4, step, 0)
+        fill(x)
+        spread_out(x, 1, fsend2.at[h], frecv2.at[h], zsend, zrecv.at[2 + h])
+        pltpu.make_async_copy(fsend2.at[h, dp], frecv2.at[h, dp], zrecv.at[2 + h]).start()
+
+    for kind in range(4):
+        if kind == 1:
+            forward(kind)
+        elif kind > 1:
+            forward2(kind - 2)
         if kind == 0:
             copies[2].wait()
             copies[3].wait()
@@ -188,12 +262,7 @@
             small = jnp.where(hit, kindv, 0.0).astype(BF16)
             msend[...] = mm(owner, small, 1, 1).reshape(NDP, 1, 128)
 
-            def meta_out(k, carry):
-                spread_out(lax.rem(base + k, GRP), msend, mrecv, zmsend, zmrecv)
-                return carry
-
-            lax.fori_loop(1, GRP + 1, meta_out, 0)
-            pltpu.make_async_copy(msend.at[dp], mrecv.at[dp], zmrecv).start()
+            everyone(msend, mrecv, zmsend, zmrecv)
 
     for t in range(NY):
         col = mm(eye, meta_r[t].astype(BF16), 1, 1)
@@ -209,6 +278,50 @@
                 return carry
 
             lax.fori_loop(0, 2 * ROWS // HD, gather_block, 0)
+
+    own_col = mm(eye, jnp.broadcast_to(prow, (8, TOK)).astype(BF16), 1, 1)[:, 0:1] * (2.0 * SLOT)
+    own_col = (own_col + mm(eye, jnp.broadcast_to(rank, (8, TOK)).astype(BF16), 1, 1)[:, 0:1]).astype(jnp.int32)
+
+    def kgather_block(b, carry):
+        r = iota((TOK, HD), 1) + b * HD
+        at = pl.ds(pl.multiple_of(b * HD, HD), HD)
+        for cb in range(8):
+            kgather[cb * TOK : (cb + 1) * TOK, at] = (r == own_col + CAP * cb).astype(F32).astype(BF16)
+        return carry
+
+    lax.fori_loop(0, 2 * ROWS // HD, kgather_block, 0)
+
+    def by_head(r):
+        return (lax.rem(r, 24) // 3) * 24 + (r // 48) * 6 + (lax.rem(r, 48) // 24) * 3 + lax.rem(r, 3)
+
+    def by_ctx(r):
+        return (lax.rem(r, 12) // 3) * 48 + (r // 96) * 24 + (lax.rem(r, 96) // 12) * 3 + lax.rem(r, 3)
+
+    ia, ib = iota((192, 192), 0), iota((192, 192), 1)
+    head_out = (ib == by_head(ia)).astype(F32).astype(BF16)
+    head_in = (ia == by_head(ib)).astype(F32).astype(BF16)
+    ctx_out = (ib == by_ctx(ia)).astype(F32).astype(BF16)
+    ctx_in = (ia == by_ctx(ib)).astype(F32).astype(BF16)
+
+    def exchange(src, dst, rsem):
+        for t in ring_y:
+            pltpu.make_async_remote_copy(
+                src_ref=src.at[t], dst_ref=dst.at[y], send_sem=kysend, recv_sem=rsem,
+                device_id=(dp, t), device_id_type=MESH,
+            ).start()
+        pltpu.make_async_copy(src.at[y], dst.at[y], rsem).start()
+
+    pltpu.make_async_copy(frecv.at[0], frecv.at[0], zrecv.at[0]).wait()
+
+    def deal(b, carry):
+        got = mm(head_out, frecv[0, pl.ds(b * GRP, GRP)].reshape(192, 128), 1, 0).astype(BF16)
+        at = pl.ds(pl.multiple_of(b * 48, 48), 48)
+        for t in range(NY):
+            ksend[t, at, :] = got[48 * t : 48 * t + 48]
+        return carry
+
+    lax.fori_loop(0, NDP // GRP, deal, 0)
+    exchange(ksend, krecv, kyrecv.at[0])
 
     a, b = iota((192, 192), 0), iota((192, 192), 1)
     split = (b == (lax.rem(a, 96) // 12) * 24 + (a // 96) * 12 + lax.rem(a, 12)).astype(F32).astype(BF16)
@@ -224,10 +337,9 @@
     pick16 = (iota((8, 128), 1) // 16 == iota((8, 128), 0)).astype(F32).astype(BF16)
     rowv[...] = mm(pick16, own.astype(BF16), 1, 1)
 
-    def arrive(kind):
+    def take(kind):
         pltpu.make_async_copy(frecv.at[kind], frecv.at[kind], zrecv.at[kind]).wait()
 
-    def take(kind):
         def unmix(b, carry):
             block = frecv[kind, pl.ds(b * GRP, GRP)].reshape(192, 128)
             got = mm(split, block, 1, 0).astype(BF16)
@@ -238,35 +350,63 @@
 
         lax.fori_loop(0, NDP // GRP, unmix, 0)
 
-    def give(kind, value):
+    def take2(h):
+        def unmix(b, carry):
+            here = pl.ds(b * GRP, GRP)
+            block = jnp.concatenate(
+                [frecv2[h, here, 0:3].reshape(192, 128), frecv2[h, here, 3:6].reshape(192, 128)], axis=1
+            )
+            got = mm(split, block, 1, 0).astype(BF16)
+            at = pl.ds(pl.multiple_of(b * 96, 96), 96)
+            for j in range(2):
+                xs[2 + 2 * h + j, at, 0:128] = got[0:96, 128 * j : 128 * j + 128]
+                xs[2 + 2 * h + j, at, 128:256] = got[96:192, 128 * j : 128 * j + 128]
+            return carry
+
+        lax.fori_loop(0, NDP // GRP, unmix, 0)
+
+    def halves_of(value, at):
+        v = value[at, :].astype(BF16)
+        return jnp.concatenate([v[:, 0:128], v[:, 128:256]], axis=0)
+
+    def give(kind):
         def mix(b, carry):
             at = pl.ds(pl.multiple_of(b * 96, 96), 96)
-            v = value[at, :].astype(BF16)
-            block = jnp.concatenate([v[:, 0:128], v[:, 128:256]], axis=0)
-            got = mm(join, block, 1, 0).astype(BF16)
+            got = mm(join, halves_of(dq_acc, at), 1, 0).astype(BF16)
             bsend[kind, pl.ds(b * GRP, GRP)] = got.reshape(GRP, 3, 8, 128)
             return carry
 
         lax.fori_loop(0, NDP // GRP, mix, 0)
 
-    def back(kind):
-        def send(k, carry):
-            spread_out(lax.rem(base + k, GRP), bsend.at[kind], brecv.at[kind], bsem_s, bsem_r.at[kind])
-            return carry
-
-        lax.fori_loop(1, GRP + 1, send, 0)
-        pltpu.make_async_copy(bsend.at[kind, dp], brecv.at[kind, dp], bsem_r.at[kind]).start()
-
-    for kind in range(2):
-        arrive(kind)
-        take(kind)
+    def give2():
+        def mix(b, carry):
+            at = pl.ds(pl.multiple_of(b * 96, 96), 96)
+            both = jnp.concatenate([halves_of(dq_acc, at), halves_of(dv_acc, at)], axis=1)
+            got = mm(join, both, 1, 0).astype(BF16)
+            here = pl.ds(b * GRP, GRP)
+            bsend2[here, 0:3] = got[:, 0:128].reshape(GRP, 3, 8, 128)
+            bsend2[here, 3:6] = got[:, 128:256].reshape(GRP, 3, 8, 128)
+            return carry
+
+        lax.fori_loop(0, NDP // GRP, mix, 0)
+
+    take(1)
+    pltpu.make_async_copy(krecv, krecv, kyrecv.at[0]).wait()
+
+    def collect(b, carry):
+        at = pl.ds(pl.multiple_of(b * 48, 48), 48)
+        got = mm(ctx_out, jnp.concatenate([krecv[t, at, :] for t in range(NY)], axis=0), 1, 0).astype(BF16)
+        at = pl.ds(pl.multiple_of(b * 96, 96), 96)
+        xs[0, at, 0:128] = got[0:96]
+        xs[0, at, 128:256] = got[96:192]
+        return carry
+
+    lax.fori_loop(0, NDP // GRP, collect, 0)
     for g in range(2):
-        arrive(2 + 2 * g)
-        take(2 + 2 * g)
-        arrive(3 + 2 * g)
+        pltpu.make_async_copy(frecv2.at[g], frecv2.at[g], zrecv.at[2 + g]).wait()
         if g == 1:
-            back(0)
-        take(3 + 2 * g)
+            everyone(bsend.at[0], brecv.at[0], bsem_s, bsem_r.at[0])
+        take2(g)
 
         def attend(b, carry):
             at = pl.ds(pl.multiple_of(b * HD, HD), HD)
@@ -296,31 +436,59 @@
             dv_acc[...] = jnp.zeros((ROWS, HD), F32)
             dk_acc[...] = jnp.zeros((ROWS, HD), F32)
         lax.fori_loop(0, ROWS // HD, attend, 0)
-        give(g, dq_acc)
-    back(1)
-    dk_acc[...] = dk_acc[...] * SCALE
-    give(2, dk_acc)
-    back(2)
-    give(3, dv_acc)
-    back(3)
-
-    for kind in range(NB):
-        pltpu.make_async_copy(brecv.at[kind], brecv.at[kind], bsem_r.at[kind]).wait()
-        got = mm(gather[...], brecv[kind].reshape(2 * ROWS, 128), 1, 0).astype(BF16)
+        if g == 0:
+            give(0)
+    def deal_back(b, carry):
+        at = pl.ds(pl.multiple_of(b * 96, 96), 96)
+        v = (dk_acc[at, :] * SCALE).astype(BF16)
+        got = mm(ctx_in, jnp.concatenate([v[:, 0:128], v[:, 128:256]], axis=0), 1, 0).astype(BF16)
+        at = pl.ds(pl.multiple_of(b * 48, 48), 48)
+        for t in range(NY):
+            dksend[t, at, :] = got[48 * t : 48 * t + 48]
+        return carry
+
+    lax.fori_loop(0, NDP // GRP, deal_back, 0)
+    exchange(dksend, dkrecv, kyrecv.at[1])
+    give2()
+    everyone(bsend2, brecv2, bsem_s, bsem_r.at[1])
+    pltpu.make_async_copy(dkrecv, dkrecv, kyrecv.at[1]).wait()
+
+    def collect_back(b, carry):
+        at = pl.ds(pl.multiple_of(b * 48, 48), 48)
+        got = mm(head_in, jnp.concatenate([dkrecv[t, at, :] for t in range(NY)], axis=0), 1, 0).astype(BF16)
+        bsend[1, pl.ds(b * GRP, GRP)] = got.reshape(GRP, 3, 8, 128)
+        return carry
+
+    lax.fori_loop(0, NDP // GRP, collect_back, 0)
+    everyone(bsend.at[1], brecv.at[1], bsem_s, bsem_r.at[2])
+
+    def home(kind, got, ref, col, sem):
         for t in range(NY):
             obuf[kind, t, :, 0:128] = got[t * TOK : (t + 1) * TOK]
             obuf[kind, t, :, 128:256] = got[(NY + t) * TOK : (NY + t + 1) * TOK]
-        ref = (oq_ref, oq_ref, ok_ref, ov_ref)[kind]
-        if kind < 2:
-            cols = pl.ds(pl.multiple_of(y * 2 * HD + kind * HD, HD), HD)
-        else:
-            cols = pl.ds(pl.multiple_of(y * HD, HD), HD)
+        cols = pl.ds(pl.multiple_of(col, HD), HD)
         for t in ring_y:
             pltpu.make_async_remote_copy(
-                src_ref=obuf.at[kind, t], dst_ref=ref.at[:, cols], send_sem=osem_s, recv_sem=osem_r.at[max(0, kind - 1)],
+                src_ref=obuf.at[kind, t], dst_ref=ref.at[:, cols], send_sem=osem_s, recv_sem=sem,
                 device_id=(dp, t), device_id_type=MESH,
             ).start()
-        pltpu.make_async_copy(obuf.at[kind, y], ref.at[:, cols], osem_r.at[max(0, kind - 1)]).start()
+        pltpu.make_async_copy(obuf.at[kind, y], ref.at[:, cols], sem).start()
+
+    pltpu.make_async_copy(brecv.at[0], brecv.at[0], bsem_r.at[0]).wait()
+    got = mm(gather[...], brecv[0].reshape(2 * ROWS, 128), 1, 0).astype(BF16)
+    home(0, got, oq_ref, y * 2 * HD, osem_r.at[0])
+    pltpu.make_async_copy(brecv2, brecv2, bsem_r.at[1]).wait()
+    both = jnp.concatenate(
+        [brecv2[:, 0:3].reshape(2 * ROWS, 128), brecv2[:, 3:6].reshape(2 * ROWS, 128)], axis=1
+    )
+    got = mm(gather[...], both, 1, 0).astype(BF16)
+    home(1, got[:, 0:128], oq_ref, y * 2 * HD + HD, osem_r.at[0])
+    home(2, got[:, 128:256], ov_ref, y * HD, osem_r.at[2])
+    pltpu.make_async_copy(brecv.at[1], brecv.at[1], bsem_r.at[2]).wait()
+    got = mm(kgather[...], brecv[1].reshape(2 * ROWS, 128), 1, 0).astype(BF16)
+    for cb in range(8):
+        kv[:, cb * TOK : (cb + 1) * TOK] = got[cb * TOK : (cb + 1) * TOK]
+    pltpu.make_async_copy(kv, ok_ref, osem_r.at[1]).start()
 
     pltpu.make_async_copy(oq_ref, oq_ref, osem_r.at[0]).wait()
     pltpu.make_async_copy(ok_ref, ok_ref, osem_r.at[1]).wait()
@@ -328,12 +496,16 @@
     some = pl.ds(0, NY - 1)
     pltpu.make_async_copy(meta_r.at[some], meta_r.at[some], ymsend).wait()
     pltpu.make_async_copy(del_r.at[some], del_r.at[some], ydsend).wait()
-    pltpu.make_async_copy(tok.at[:, some], tok.at[:, some], ysend).wait()
-    pltpu.make_async_copy(obuf.at[:, some], obuf.at[:, some], osem_s).wait()
+    pltpu.make_async_copy(tok.at[1:NT, some], tok.at[1:NT, some], ysend).wait()
+    pltpu.make_async_copy(ksend.at[some], ksend.at[some], kysend).wait()
+    pltpu.make_async_copy(dksend.at[some], dksend.at[some], kysend).wait()
+    pltpu.make_async_copy(obuf.at[0:3, some], obuf.at[0:3, some], osem_s).wait()
     most = pl.ds(0, NDP - 1)
     pltpu.make_async_copy(msend.at[most], msend.at[most], zmsend).wait()
     pltpu.make_async_copy(fsend.at[:, most], fsend.at[:, most], zsend).wait()
+    pltpu.make_async_copy(fsend2.at[:, most], fsend2.at[:, most], zsend).wait()
     pltpu.make_async_copy(bsend.at[:, most], bsend.at[:, most], bsem_s).wait()
+    pltpu.make_async_copy(bsend2.at[most], bsend2.at[most], bsem_s).wait()
 
 
 def body(queries, key_rows, values, saved_out, out_grad, pack_of, segment_label):
@@ -360,8 +532,8 @@
             pltpu.VMEM((NY, 8, TOK), F32),
             pltpu.VMEM((2 * ROWS, 2 * NY * TOK), BF16),
             pltpu.VMEM((2 * NY * TOK, 2 * ROWS), BF16),
-            pltpu.VMEM((NT, NDP, 3, 8, 128), BF16),
-            pltpu.VMEM((NT, NDP, 3, 8, 128), BF16),
+            pltpu.VMEM((2, NDP, 3, 8, 128), BF16),
+            pltpu.VMEM((2, NDP, 3, 8, 128), BF16),
             pltpu.VMEM((NDP, 1, 128), F32),
             pltpu.VMEM((NDP, 1, 128), F32),
             pltpu.VMEM((NT, ROWS, HD), BF16),
@@ -370,15 +542,26 @@
             pltpu.VMEM((ROWS, HD), F32),
             pltpu.VMEM((ROWS, HD), F32),
             pltpu.VMEM((ROWS, HD), F32),
-            pltpu.VMEM((NB, NDP, 3, 8, 128), BF16),
-            pltpu.VMEM((NB, NDP, 3, 8, 128), BF16),
+            pltpu.VMEM((2, NDP, 3, 8, 128), BF16),
+            pltpu.VMEM((2, NDP, 3, 8, 128), BF16),
             pltpu.VMEM((NB, NY, TOK, HD), BF16),
-            dma((2,)), dma((2,)), dma, dma((NT,)), dma, dma, dma, dma, dma, dma((NT,)), dma, dma,
-            dma, dma((NB,)), dma, dma((3,)),
+            pltpu.VMEM((2, NDP, 6, 8, 128), BF16),
+            pltpu.VMEM((2, NDP, 6, 8, 128), BF16),
+            pltpu.VMEM((NDP, 6, 8, 128), BF16),
+            pltpu.VMEM((NDP, 6, 8, 128), BF16),
+            pltpu.VMEM((TOK, 4 * HD), BF16),
+            pltpu.VMEM((2 * ROWS, 8 * TOK), BF16),
+            pltpu.VMEM((8 * TOK, 2 * ROWS), BF16),
+            pltpu.VMEM((NY, 2 * 192, 128), BF16),
+            pltpu.VMEM((NY, 2 * 192, 128), BF16),
+            pltpu.VMEM((NY, 2 * 192, 128), BF16),
+            pltpu.VMEM((NY, 2 * 192, 128), BF16),
+            dma, dma, dma((2,)), dma((2,)), dma((2,)), dma, dma((NT,)), dma, dma, dma, dma, dma, dma((4,)), dma, dma,
+            dma, dma((3,)), dma, dma((3,)),
             pltpu.SemaphoreType.REGULAR, pltpu.SemaphoreType.REGULAR,
         ],
         compiler_params=pltpu.CompilerParams(
-            collective_id=0, has_side_effects=True, vmem_limit_bytes=52 << 20
+            collective_id=0, has_side_effects=True, vmem_limit_bytes=63 << 20
         ),
         name="packed_attention_backward",
     )(

time: 118 us -> 114 us (0.966)
  Pallas kernels: 112 us -> 110 us
    pallas_call x1, Pallas kernels: 112 us -> 110 us  [body(): pl.pallas_call(kernel, out_shape=(jax.ShapeDtypeStruct((TOK, 8 * HD), BF1...]
    unnamed x11 -> x7, local copies, waits for them, and re-layouts: 4.75 us -> 3.67 us
where the time goes in v3:
time: 114 us
  Pallas kernels  110 us (96%)
  local copies, waits for them, and re-layouts  3.67 us (3%)
    pallas_call x1, Pallas kernels, body(): pl.pallas_call(kernel, out_shape=(jax.ShapeDtypeStruct((TOK, 8 * HD), BF1...  110 us
    unnamed x7, local copies, waits for them, and re-layouts  3.67 us

profile of v3, /device:TPU:1, one launch (start us, length us, event | category | flops | bytes accessed | tf_op | source)
XLA Modules:
  0.0 113.9 jit_solution(6388101938890288642)
XLA Ops:
  0.6 109.6 %packed_attention_backward.1 = (bf16[128,2048]{1,0:T(8,128)(2,1)}, bf16[128,1024]{1,0:T(8,128)(2,1)}, bf16[128,1024]{1,0:T(8,128)(2,1)}) custom-call(bf16[128,2048]{1,0:T(8,128)(2,1)} %q_ref.1, bf16[128,1024]{1,0:T(8,128)(2,1)} %k_ref.1, bf16[128,1024]{1,0:T(8,128)(2,1)} %v_ref.1, bf16[128,2048]{1,0:T(8,128)(2,1)} %g_ref.1, bf16[128,2048]{1,0:T(8,128)(2,1)} %o_ref.1, ...), custom_call_target="tpu_custom_call" | custom-call | tf_op jit(solution)/shard_map/packed_attention_backward/pallas_call | solution.py:515
  110.2 0.0 copy-start.1
  110.2 1.9 %copy.13 = bf16[128,2048]{1,0:T(8,128)(2,1)} copy(bf16[128,2048]{1,0:T(8,128)(2,1)} %get-tuple-element.6) | data formatting | bytes 1048576
  112.2 0.0 copy-done.1
  112.2 0.0 copy-start
  112.2 0.7 copy.14
  112.9 0.3 copy-done
  113.2 0.7 copy.15
Async XLA Ops:
  110.2 1.9 %copy-start.1 = (bf16[128,1024]{1,0:T(8,128)(2,1)S(1)}, bf16[128,1024]{1,0:T(8,128)(2,1)}, u32[]{:S(2)}) copy-start(bf16[128,1024]{1,0:T(8,128)(2,1)} %get-tuple-element.7) | copy-start | bytes 786436
  112.2 1.0 copy-start

commit v4 on v3

--- a/solution.py
+++ b/solution.py
@@ -18,10 +18,11 @@
 ROWS = NDP * SLOT
 GRP = 8
 PLANE = 16
+EARLY = 3
 MASKED = -1e30
 SCALE = 1.0 / 16.0
 
-NT, NB = 6, 4
+NT = 6
 
 
 def iota(shape, dim):
@@ -36,7 +37,7 @@
     q_ref, k_ref, v_ref, g_ref, o_ref, pack_ref, lab_ref,
     oq_ref, ok_ref, ov_ref,
     ints, gv, ov, tok, meta_s, meta_r, del_s, del_r, place, gather, fsend, frecv, msend, mrecv, xs, rowv, labk,
-    dq_acc, dk_acc, dv_acc, bsend, brecv, obuf, fsend2, frecv2, bsend2, brecv2,
+    dq_acc, dk_acc, dv_acc, bsend, brecv, obuf, fsend2, frecv2, kvout,
     kv, kplace, kgather, ksend, krecv, dksend, dkrecv,
     ksem, kysend, kyrecv, insem, isem, ysend, yrecv, ymsend, ymrecv, ydsend, ydrecv, zsend, zrecv, zmsend, zmrecv,
     bsem_s, bsem_r, osem_s, osem_r, plane_sem, core_sem,
@@ -98,6 +99,9 @@
 
     pl.semaphore_wait(bar, 14)
 
+    for d in ring_x:
+        greet(plane_sem, d, y)
+
     for t in ring_y:
         pltpu.make_async_remote_copy(
             src_ref=meta_s, dst_ref=meta_r.at[y], send_sem=ymsend, recv_sem=ymrecv,
@@ -110,12 +114,6 @@
                 device_id=(dp, t), device_id_type=MESH,
             ).start()
 
-    for d in ring_x:
-        greet(plane_sem, d, y)
-    pl.semaphore_wait(plane_sem, 3)
-    greet(core_sem, other, y)
-    pl.semaphore_wait(core_sem, 1)
-
     own_row = (prow * (2.0 * SLOT) + rank).astype(jnp.int32)
 
     def kplace_block(b, carry):
@@ -126,6 +124,9 @@
         return carry
 
     lax.fori_loop(0, 2 * ROWS // HD, kplace_block, 0)
+
+    pl.semaphore_wait(plane_sem, 3)
+    greet(core_sem, other, y)
 
     spin = [lax.rem(dp + j, PLANE) for j in range(PLANE)]
 
@@ -149,12 +150,13 @@
         fsend[0, pl.ds(g * PLANE, PLANE)] = got.astype(BF16).reshape(PLANE, 3, 8, 128)
 
     def step_k(k, carry):
-        fill_k(plane(k))
         spread_out(plane(k), 0, fsend.at[0], frecv.at[0], zsend, zrecv.at[0])
+        fill_k(plane(k + 1))
         return carry
 
+    fill_k(plane(1))
+    pl.semaphore_wait(core_sem, 1)
     lax.fori_loop(1, 4, step_k, 0)
-    fill_k(x)
     spread_out(x, 1, fsend.at[0], frecv.at[0], zsend, zrecv.at[0])
     pltpu.make_async_copy(fsend.at[0, dp], frecv.at[0, dp], zrecv.at[0]).start()
 
@@ -172,12 +174,12 @@
 
     lax.fori_loop(0, 2 * ROWS // HD, place_block, 0)
 
-    def everyone(src, dst, ssem, rsem):
+    def everyone(src, dst, ssem, rsem, done=0):
         def send(k, carry):
             spread_out(plane(k), 0, src, dst, ssem, rsem)
             return carry
 
-        lax.fori_loop(1, 4, send, 0)
+        lax.fori_loop(1 + done, 4, send, 0)
         spread_out(x, 1, src, dst, ssem, rsem)
         pltpu.make_async_copy(src.at[dp], dst.at[dp], rsem).start()
 
@@ -229,7 +231,7 @@
         spread_out(x, 1, fsend2.at[h], frecv2.at[h], zsend, zrecv.at[2 + h])
         pltpu.make_async_copy(fsend2.at[h, dp], frecv2.at[h, dp], zrecv.at[2 + h]).start()
 
-    for kind in range(4):
+    for kind in range(3):
         if kind == 1:
             forward(kind)
         elif kind > 1:
@@ -322,6 +324,7 @@
 
     lax.fori_loop(0, NDP // GRP, deal, 0)
     exchange(ksend, krecv, kyrecv.at[0])
+    forward2(1)
 
     a, b = iota((192, 192), 0), iota((192, 192), 1)
     split = (b == (lax.rem(a, 96) // 12) * 24 + (a // 96) * 12 + lax.rem(a, 12)).astype(F32).astype(BF16)
@@ -365,27 +368,12 @@
 
         lax.fori_loop(0, NDP // GRP, unmix, 0)
 
-    def halves_of(value, at):
-        v = value[at, :].astype(BF16)
-        return jnp.concatenate([v[:, 0:128], v[:, 128:256]], axis=0)
-
     def give(kind):
         def mix(b, carry):
             at = pl.ds(pl.multiple_of(b * 96, 96), 96)
-            got = mm(join, halves_of(dq_acc, at), 1, 0).astype(BF16)
+            v = dq_acc[at, :].astype(BF16)
+            got = mm(join, jnp.concatenate([v[:, 0:128], v[:, 128:256]], axis=0), 1, 0).astype(BF16)
             bsend[kind, pl.ds(b * GRP, GRP)] = got.reshape(GRP, 3, 8, 128)
-            return carry
-
-        lax.fori_loop(0, NDP // GRP, mix, 0)
-
-    def give2():
-        def mix(b, carry):
-            at = pl.ds(pl.multiple_of(b * 96, 96), 96)
-            both = jnp.concatenate([halves_of(dq_acc, at), halves_of(dv_acc, at)], axis=1)
-            got = mm(join, both, 1, 0).astype(BF16)
-            here = pl.ds(b * GRP, GRP)
-            bsend2[here, 0:3] = got[:, 0:128].reshape(GRP, 3, 8, 128)
-            bsend2[here, 3:6] = got[:, 128:256].reshape(GRP, 3, 8, 128)
             return carry
 
         lax.fori_loop(0, NDP // GRP, mix, 0)
@@ -403,9 +391,12 @@
 
     lax.fori_loop(0, NDP // GRP, collect, 0)
     for g in range(2):
+        if g == 1:
+            for k in range(EARLY):
+                spread_out(plane(1 + k), 0, bsend.at[0], brecv.at[0], bsem_s, bsem_r.at[0])
         pltpu.make_async_copy(frecv2.at[g], frecv2.at[g], zrecv.at[2 + g]).wait()
         if g == 1:
-            everyone(bsend.at[0], brecv.at[0], bsem_s, bsem_r.at[0])
+            everyone(bsend.at[0], brecv.at[0], bsem_s, bsem_r.at[0], EARLY)
         take2(g)
 
         def attend(b, carry):
@@ -436,31 +427,22 @@
             dv_acc[...] = jnp.zeros((ROWS, HD), F32)
             dk_acc[...] = jnp.zeros((ROWS, HD), F32)
         lax.fori_loop(0, ROWS // HD, attend, 0)
-        if g == 0:
-            give(0)
-    def deal_back(b, carry):
-        at = pl.ds(pl.multiple_of(b * 96, 96), 96)
-        v = (dk_acc[at, :] * SCALE).astype(BF16)
-        got = mm(ctx_in, jnp.concatenate([v[:, 0:128], v[:, 128:256]], axis=0), 1, 0).astype(BF16)
-        at = pl.ds(pl.multiple_of(b * 48, 48), 48)
-        for t in range(NY):
-            dksend[t, at, :] = got[48 * t : 48 * t + 48]
-        return carry
-
-    lax.fori_loop(0, NDP // GRP, deal_back, 0)
-    exchange(dksend, dkrecv, kyrecv.at[1])
-    give2()
-    everyone(bsend2, brecv2, bsem_s, bsem_r.at[1])
-    pltpu.make_async_copy(dkrecv, dkrecv, kyrecv.at[1]).wait()
-
-    def collect_back(b, carry):
-        at = pl.ds(pl.multiple_of(b * 48, 48), 48)
-        got = mm(head_in, jnp.concatenate([dkrecv[t, at, :] for t in range(NY)], axis=0), 1, 0).astype(BF16)
-        bsend[1, pl.ds(b * GRP, GRP)] = got.reshape(GRP, 3, 8, 128)
-        return carry
-
-    lax.fori_loop(0, NDP // GRP, collect_back, 0)
-    everyone(bsend.at[1], brecv.at[1], bsem_s, bsem_r.at[2])
+        give(g)
+    everyone(bsend.at[1], brecv.at[1], bsem_s, bsem_r.at[1])
+
+    for n, acc in enumerate((dk_acc, dv_acc)):
+
+        def deal_back(b, carry):
+            at = pl.ds(pl.multiple_of(b * 96, 96), 96)
+            v = (acc[at, :] * SCALE if n == 0 else acc[at, :]).astype(BF16)
+            got = mm(ctx_in, jnp.concatenate([v[:, 0:128], v[:, 128:256]], axis=0), 1, 0).astype(BF16)
+            at = pl.ds(pl.multiple_of(b * 48, 48), 48)
+            for t in range(NY):
+                dksend[n, t, at, :] = got[48 * t : 48 * t + 48]
+            return carry
+
+        lax.fori_loop(0, NDP // GRP, deal_back, 0)
+        exchange(dksend.at[n], dkrecv.at[n], kyrecv.at[1 + n])
 
     def home(kind, got, ref, col, sem):
         for t in range(NY):
@@ -474,21 +456,30 @@
             ).start()
         pltpu.make_async_copy(obuf.at[kind, y], ref.at[:, cols], sem).start()
 
-    pltpu.make_async_copy(brecv.at[0], brecv.at[0], bsem_r.at[0]).wait()
-    got = mm(gather[...], brecv[0].reshape(2 * ROWS, 128), 1, 0).astype(BF16)
-    home(0, got, oq_ref, y * 2 * HD, osem_r.at[0])
-    pltpu.make_async_copy(brecv2, brecv2, bsem_r.at[1]).wait()
-    both = jnp.concatenate(
-        [brecv2[:, 0:3].reshape(2 * ROWS, 128), brecv2[:, 3:6].reshape(2 * ROWS, 128)], axis=1
-    )
-    got = mm(gather[...], both, 1, 0).astype(BF16)
-    home(1, got[:, 0:128], oq_ref, y * 2 * HD + HD, osem_r.at[0])
-    home(2, got[:, 128:256], ov_ref, y * HD, osem_r.at[2])
-    pltpu.make_async_copy(brecv.at[1], brecv.at[1], bsem_r.at[2]).wait()
-    got = mm(kgather[...], brecv[1].reshape(2 * ROWS, 128), 1, 0).astype(BF16)
-    for cb in range(8):
-        kv[:, cb * TOK : (cb + 1) * TOK] = got[cb * TOK : (cb + 1) * TOK]
-    pltpu.make_async_copy(kv, ok_ref, osem_r.at[1]).start()
+    def home_q(g):
+        pltpu.make_async_copy(brecv.at[g], brecv.at[g], bsem_r.at[g]).wait()
+        got = mm(gather[...], brecv[g].reshape(2 * ROWS, 128), 1, 0).astype(BF16)
+        home(g, got, oq_ref, y * 2 * HD + g * HD, osem_r.at[0])
+
+    home_q(0)
+    for n in range(2):
+        pltpu.make_async_copy(dkrecv.at[n], dkrecv.at[n], kyrecv.at[1 + n]).wait()
+
+        def collect_back(b, carry):
+            at = pl.ds(pl.multiple_of(b * 48, 48), 48)
+            got = mm(head_in, jnp.concatenate([dkrecv[n, t, at, :] for t in range(NY)], axis=0), 1, 0).astype(BF16)
+            bsend[2 + n, pl.ds(b * GRP, GRP)] = got.reshape(GRP, 3, 8, 128)
+            return carry
+
+        lax.fori_loop(0, NDP // GRP, collect_back, 0)
+        everyone(bsend.at[2 + n], brecv.at[2 + n], bsem_s, bsem_r.at[2 + n])
+    home_q(1)
+    for n, ref in enumerate((ok_ref, ov_ref)):
+        pltpu.make_async_copy(brecv.at[2 + n], brecv.at[2 + n], bsem_r.at[2 + n]).wait()
+        got = mm(kgather[...], brecv[2 + n].reshape(2 * ROWS, 128), 1, 0).astype(BF16)
+        for cb in range(8):
+            kvout[n, :, cb * TOK : (cb + 1) * TOK] = got[cb * TOK : (cb + 1) * TOK]
+        pltpu.make_async_copy(kvout.at[n], ref, osem_r.at[1 + n]).start()
 
     pltpu.make_async_copy(oq_ref, oq_ref, osem_r.at[0]).wait()
     pltpu.make_async_copy(ok_ref, ok_ref, osem_r.at[1]).wait()
@@ -498,27 +489,29 @@
     pltpu.make_async_copy(del_r.at[some], del_r.at[some], ydsend).wait()
     pltpu.make_async_copy(tok.at[1:NT, some], tok.at[1:NT, some], ysend).wait()
     pltpu.make_async_copy(ksend.at[some], ksend.at[some], kysend).wait()
-    pltpu.make_async_copy(dksend.at[some], dksend.at[some], kysend).wait()
-    pltpu.make_async_copy(obuf.at[0:3, some], obuf.at[0:3, some], osem_s).wait()
+    pltpu.make_async_copy(dksend.at[:, some], dksend.at[:, some], kysend).wait()
+    pltpu.make_async_copy(obuf.at[:, some], obuf.at[:, some], osem_s).wait()
     most = pl.ds(0, NDP - 1)
     pltpu.make_async_copy(msend.at[most], msend.at[most], zmsend).wait()
     pltpu.make_async_copy(fsend.at[:, most], fsend.at[:, most], zsend).wait()
     pltpu.make_async_copy(fsend2.at[:, most], fsend2.at[:, most], zsend).wait()
     pltpu.make_async_copy(bsend.at[:, most], bsend.at[:, most], bsem_s).wait()
-    pltpu.make_async_copy(bsend2.at[most], bsend2.at[most], bsem_s).wait()
+
+
+def settle(a_ref, b_ref, c_ref, oa_ref, ob_ref, oc_ref):
+    oa_ref[...] = a_ref[...]
+    ob_ref[...] = b_ref[...]
+    oc_ref[...] = c_ref[...]
 
 
 def body(queries, key_rows, values, saved_out, out_grad, pack_of, segment_label):
     anywhere = pl.BlockSpec(memory_space=pl.ANY)
     hbm = pl.BlockSpec(memory_space=pltpu.HBM)
     dma = pltpu.SemaphoreType.DMA
-    return pl.pallas_call(
+    shapes = tuple(jax.ShapeDtypeStruct((TOK, n * HD), BF16) for n in (8, 4, 4))
+    grads = pl.pallas_call(
         kernel,
-        out_shape=(
-            jax.ShapeDtypeStruct((TOK, 8 * HD), BF16),
-            jax.ShapeDtypeStruct((TOK, 4 * HD), BF16),
-            jax.ShapeDtypeStruct((TOK, 4 * HD), BF16),
-        ),
+        out_shape=shapes,
         in_specs=[hbm] * 7,
         out_specs=(anywhere,) * 3,
         scratch_shapes=[
@@ -542,22 +535,21 @@
             pltpu.VMEM((ROWS, HD), F32),
             pltpu.VMEM((ROWS, HD), F32),
             pltpu.VMEM((ROWS, HD), F32),
-            pltpu.VMEM((2, NDP, 3, 8, 128), BF16),
-            pltpu.VMEM((2, NDP, 3, 8, 128), BF16),
-            pltpu.VMEM((NB, NY, TOK, HD), BF16),
+            pltpu.VMEM((4, NDP, 3, 8, 128), BF16),
+            pltpu.VMEM((4, NDP, 3, 8, 128), BF16),
+            pltpu.VMEM((2, NY, TOK, HD), BF16),
             pltpu.VMEM((2, NDP, 6, 8, 128), BF16),
             pltpu.VMEM((2, NDP, 6, 8, 128), BF16),
-            pltpu.VMEM((NDP, 6, 8, 128), BF16),
-            pltpu.VMEM((NDP, 6, 8, 128), BF16),
+            pltpu.VMEM((2, TOK, 4 * HD), BF16),
             pltpu.VMEM((TOK, 4 * HD), BF16),
             pltpu.VMEM((2 * ROWS, 8 * TOK), BF16),
             pltpu.VMEM((8 * TOK, 2 * ROWS), BF16),
             pltpu.VMEM((NY, 2 * 192, 128), BF16),
             pltpu.VMEM((NY, 2 * 192, 128), BF16),
-            pltpu.VMEM((NY, 2 * 192, 128), BF16),
-            pltpu.VMEM((NY, 2 * 192, 128), BF16),
-            dma, dma, dma((2,)), dma((2,)), dma((2,)), dma, dma((NT,)), dma, dma, dma, dma, dma, dma((4,)), dma, dma,
-            dma, dma((3,)), dma, dma((3,)),
+            pltpu.VMEM((2, NY, 2 * 192, 128), BF16),
+            pltpu.VMEM((2, NY, 2 * 192, 128), BF16),
+            dma, dma, dma((3,)), dma((2,)), dma((2,)), dma, dma((NT,)), dma, dma, dma, dma, dma, dma((4,)), dma, dma,
+            dma, dma((4,)), dma, dma((3,)),
             pltpu.SemaphoreType.REGULAR, pltpu.SemaphoreType.REGULAR,
         ],
         compiler_params=pltpu.CompilerParams(
@@ -568,6 +560,13 @@
         queries, key_rows, values, out_grad, saved_out,
         pack_of.reshape(1, TOK), segment_label.reshape(1, TOK),
     )
+    return pl.pallas_call(
+        settle,
+        out_shape=shapes,
+        in_specs=[pl.BlockSpec(memory_space=pltpu.VMEM)] * 3,
+        out_specs=(pl.BlockSpec(memory_space=pltpu.VMEM),) * 3,
+        name="settle",
+    )(*grads)
 
 
 def solution(mesh):

time: 114 us -> 110 us (0.965)
  local copies, waits for them, and re-layouts: 3.67 us -> 0 us
    unnamed x7 -> x0, local copies, waits for them, and re-layouts: 3.67 us -> none
    pallas_call x1 -> x2, Pallas kernels: 110 us -> 110 us  [the longest x1 107 us: body(): pl.pallas_call(kernel, out_shape=shapes, in_specs=[hbm] * 7, out_specs=(a...]
where the time goes in v4:
time: 110 us
  Pallas kernels  110 us (100%)
    pallas_call x1, Pallas kernels, body(): pl.pallas_call(kernel, out_shape=shapes, in_specs=[hbm] * 7, out_specs=(a...  107 us

profile of v4, /device:TPU:1, one launch (start us, length us, event | category | flops | bytes accessed | tf_op | source)
XLA Modules:
  0.0 110.2 jit_solution(1021364986004507372)
XLA Ops:
  0.6 107.4 %packed_attention_backward.1 = (bf16[128,2048]{1,0:T(8,128)(2,1)}, bf16[128,1024]{1,0:T(8,128)(2,1)}, bf16[128,1024]{1,0:T(8,128)(2,1)}) custom-call(bf16[128,2048]{1,0:T(8,128)(2,1)} %q_ref.1, bf16[128,1024]{1,0:T(8,128)(2,1)} %k_ref.1, bf16[128,1024]{1,0:T(8,128)(2,1)} %v_ref.1, bf16[128,2048]{1,0:T(8,128)(2,1)} %g_ref.1, bf16[128,2048]{1,0:T(8,128)(2,1)} %o_ref.1, ...), custom_call_target="tpu_custom_call" | custom-call | tf_op jit(solution)/shard_map/packed_attention_backward/pallas_call | solution.py:512
  108.1 2.2 %settle.1 = (bf16[128,2048]{1,0:T(8,128)(2,1)}, bf16[128,1024]{1,0:T(8,128)(2,1)}, bf16[128,1024]{1,0:T(8,128)(2,1)}) custom-call(bf16[128,2048]{1,0:T(8,128)(2,1)} %get-tuple-element.6.a_ref, bf16[128,1024]{1,0:T(8,128)(2,1)} %get-tuple-element.7.b_ref, bf16[128,1024]{1,0:T(8,128)(2,1)} %get-tuple-element.8.c_ref), custom_call_target="tpu_custom_call" | custom-call | tf_op jit(solution)/shard_map/settle/pallas_call | solution.py:563

commit v5 on v4

--- a/solution.py
+++ b/solution.py
@@ -18,6 +18,7 @@
 ROWS = NDP * SLOT
 GRP = 8
 PLANE = 16
+Z_ORDER = (0, 4, 1, 5, 2, 6, 3, 7)
 EARLY = 3
 MASKED = -1e30
 SCALE = 1.0 / 16.0
@@ -38,7 +39,7 @@
     oq_ref, ok_ref, ov_ref,
     ints, gv, ov, tok, meta_s, meta_r, del_s, del_r, place, gather, fsend, frecv, msend, mrecv, xs, rowv, labk,
     dq_acc, dk_acc, dv_acc, bsend, brecv, obuf, fsend2, frecv2, kvout,
-    kv, kplace, kgather, ksend, krecv, dksend, dkrecv,
+    kv, kgather, ksend, krecv, dksend, dkrecv,
     ksem, kysend, kyrecv, insem, isem, ysend, yrecv, ymsend, ymrecv, ydsend, ydrecv, zsend, zrecv, zmsend, zmrecv,
     bsem_s, bsem_r, osem_s, osem_r, plane_sem, core_sem,
 ):
@@ -47,14 +48,24 @@
     x, z, c = dp // 16, lax.rem(dp // 2, 8), lax.rem(dp, 2)
     bar = pltpu.get_barrier_semaphore()
 
-    def at(nx, nz, nc):
+    copies = [
+        pltpu.make_async_copy(pack_ref, ints.at[0], isem.at[0]),
+        pltpu.make_async_copy(lab_ref, ints.at[1], isem.at[1]),
+        pltpu.make_async_copy(g_ref, gv, insem.at[0]),
+        pltpu.make_async_copy(o_ref, ov, insem.at[1]),
+        pltpu.make_async_copy(k_ref, kv, ksem),
+    ]
+    for n in (0, 1, 4):
+        copies[n].start()
+
+    def spot(nx, nz, nc):
         return (nx * 8 + nz) * 2 + nc
 
     def greet(sem, d, t):
         pl.semaphore_signal(sem, inc=1, device_id=(d, t), device_id_type=MESH)
 
-    ring_x = [at(lax.rem(x + j, 4), z, c) for j in range(1, 4)]
-    other = at(x, z, 1 - c)
+    ring_x = [spot(lax.rem(x + j, 4), z, c) for j in range(1, 4)]
+    other = spot(x, z, 1 - c)
     ring_y = [lax.rem(y + j, NY) for j in range(1, NY)]
     for t in ring_y:
         greet(bar, dp, t)
@@ -62,26 +73,13 @@
         greet(bar, d, y)
     greet(bar, other, y)
     for j in range(1, 8):
-        greet(bar, at(x, lax.rem(z + j, 8), c), y)
-
-    copies = [
-        pltpu.make_async_copy(pack_ref, ints.at[0], isem.at[0]),
-        pltpu.make_async_copy(lab_ref, ints.at[1], isem.at[1]),
-        pltpu.make_async_copy(g_ref, gv, insem.at[0]),
-        pltpu.make_async_copy(o_ref, ov, insem.at[1]),
-        pltpu.make_async_copy(k_ref, kv, ksem),
-    ]
-    for n in (0, 1, 4, 2, 3):
-        copies[n].start()
+        greet(bar, spot(x, lax.rem(z + j, 8), c), y)
 
     def columns(kind, head):
         if kind == 1:
             return v_ref.at[:, pl.ds(pl.multiple_of(head * HD, HD), HD)]
         ref = q_ref if kind % 2 == 0 else g_ref
         return ref.at[:, pl.ds(pl.multiple_of(head * 2 * HD + (kind // 2 - 1) * HD, HD), HD)]
-
-    for kind in range(1, NT):
-        pltpu.make_async_copy(columns(kind, y), tok.at[kind, y], yrecv.at[kind]).start()
 
     eye = (iota((TOK, TOK), 0) == iota((TOK, TOK), 1)).astype(F32).astype(BF16)
     copies[0].wait()
@@ -102,31 +100,7 @@
     for d in ring_x:
         greet(plane_sem, d, y)
 
-    for t in ring_y:
-        pltpu.make_async_remote_copy(
-            src_ref=meta_s, dst_ref=meta_r.at[y], send_sem=ymsend, recv_sem=ymrecv,
-            device_id=(dp, t), device_id_type=MESH,
-        ).start()
-    for kind in range(1, NT):
-        for t in ring_y:
-            pltpu.make_async_remote_copy(
-                src_ref=columns(kind, t), dst_ref=tok.at[kind, y], send_sem=ysend, recv_sem=yrecv.at[kind],
-                device_id=(dp, t), device_id_type=MESH,
-            ).start()
-
     own_row = (prow * (2.0 * SLOT) + rank).astype(jnp.int32)
-
-    def kplace_block(b, carry):
-        r = iota((HD, TOK), 0) + b * HD
-        at = pl.ds(pl.multiple_of(b * HD, HD), HD)
-        for cb in range(8):
-            kplace[at, cb * TOK : (cb + 1) * TOK] = (r == own_row + CAP * cb).astype(F32).astype(BF16)
-        return carry
-
-    lax.fori_loop(0, 2 * ROWS // HD, kplace_block, 0)
-
-    pl.semaphore_wait(plane_sem, 3)
-    greet(core_sem, other, y)
 
     spin = [lax.rem(dp + j, PLANE) for j in range(PLANE)]
 
@@ -141,24 +115,43 @@
                 device_id=(d, y), device_id_type=MESH,
             ).start()
 
-    copies[4].wait()
-
     def fill_k(g):
-        at = pl.ds(pl.multiple_of(g * 24 * PLANE, 24 * PLANE), 24 * PLANE)
+        r = iota((24 * PLANE, TOK), 0) + g * (24 * PLANE)
+        hot = jnp.concatenate([(r == own_row + CAP * cb).astype(F32).astype(BF16) for cb in range(8)], axis=1)
         stack = jnp.concatenate([kv[:, cb * TOK : (cb + 1) * TOK] for cb in range(8)], axis=0)
-        got = mm(kplace[at, :], stack, 1, 0)
-        fsend[0, pl.ds(g * PLANE, PLANE)] = got.astype(BF16).reshape(PLANE, 3, 8, 128)
+        fsend[0, pl.ds(g * PLANE, PLANE)] = mm(hot, stack, 1, 0).astype(BF16).reshape(PLANE, 3, 8, 128)
 
     def step_k(k, carry):
         spread_out(plane(k), 0, fsend.at[0], frecv.at[0], zsend, zrecv.at[0])
         fill_k(plane(k + 1))
         return carry
 
+    def columns_out(kind):
+        for t in ring_y:
+            pltpu.make_async_remote_copy(
+                src_ref=columns(kind, t), dst_ref=tok.at[kind, y], send_sem=ysend, recv_sem=yrecv.at[kind],
+                device_id=(dp, t), device_id_type=MESH,
+            ).start()
+        pltpu.make_async_copy(columns(kind, y), tok.at[kind, y], yrecv.at[kind]).start()
+
+    copies[4].wait()
     fill_k(plane(1))
+    pl.semaphore_wait(plane_sem, 3)
+    greet(core_sem, other, y)
+    for t in ring_y:
+        pltpu.make_async_remote_copy(
+            src_ref=meta_s, dst_ref=meta_r.at[y], send_sem=ymsend, recv_sem=ymrecv,
+            device_id=(dp, t), device_id_type=MESH,
+        ).start()
+    columns_out(1)
     pl.semaphore_wait(core_sem, 1)
     lax.fori_loop(1, 4, step_k, 0)
     spread_out(x, 1, fsend.at[0], frecv.at[0], zsend, zrecv.at[0])
     pltpu.make_async_copy(fsend.at[0, dp], frecv.at[0, dp], zrecv.at[0]).start()
+    copies[2].start()
+    copies[3].start()
+    for kind in range(2, NT):
+        columns_out(kind)
 
     pltpu.make_async_copy(meta_r.at[pl.ds(0, NY - 1)], meta_r.at[pl.ds(0, NY - 1)], ymrecv).wait()
     packs = jnp.concatenate([meta_r[t, 0:1, :] for t in range(NY)], axis=1)
@@ -181,6 +174,20 @@
 
         lax.fori_loop(1 + done, 4, send, 0)
         spread_out(x, 1, src, dst, ssem, rsem)
+        pltpu.make_async_copy(src.at[dp], dst.at[dp], rsem).start()
+
+    def by_z(src, dst, ssem, rsem):
+        for nz in Z_ORDER:
+            for j in range(8):
+                d = spot(lax.rem(x + 1 + j // 2, 4), nz, j % 2)
+
+                @pl.when(d != dp)
+                def _():
+                    pltpu.make_async_remote_copy(
+                        src_ref=src.at[d], dst_ref=dst.at[dp], send_sem=ssem, recv_sem=rsem,
+                        device_id=(d, y), device_id_type=MESH,
+                    ).start()
+
         pltpu.make_async_copy(src.at[dp], dst.at[dp], rsem).start()
 
     def landed(kind):
@@ -427,11 +434,10 @@
             dv_acc[...] = jnp.zeros((ROWS, HD), F32)
             dk_acc[...] = jnp.zeros((ROWS, HD), F32)
         lax.fori_loop(0, ROWS // HD, attend, 0)
-        give(g)
-    everyone(bsend.at[1], brecv.at[1], bsem_s, bsem_r.at[1])
-
-    for n, acc in enumerate((dk_acc, dv_acc)):
-
+        if g == 0:
+            give(0)
+
+    def deal_out(n, acc):
         def deal_back(b, carry):
             at = pl.ds(pl.multiple_of(b * 96, 96), 96)
             v = (acc[at, :] * SCALE if n == 0 else acc[at, :]).astype(BF16)
@@ -443,6 +449,11 @@
 
         lax.fori_loop(0, NDP // GRP, deal_back, 0)
         exchange(dksend.at[n], dkrecv.at[n], kyrecv.at[1 + n])
+
+    deal_out(0, dk_acc)
+    give(1)
+    everyone(bsend.at[1], brecv.at[1], bsem_s, bsem_r.at[1])
+    deal_out(1, dv_acc)
 
     def home(kind, got, ref, col, sem):
         for t in range(NY):
@@ -461,7 +472,6 @@
         got = mm(gather[...], brecv[g].reshape(2 * ROWS, 128), 1, 0).astype(BF16)
         home(g, got, oq_ref, y * 2 * HD + g * HD, osem_r.at[0])
 
-    home_q(0)
     for n in range(2):
         pltpu.make_async_copy(dkrecv.at[n], dkrecv.at[n], kyrecv.at[1 + n]).wait()
 
@@ -472,8 +482,8 @@
             return carry
 
         lax.fori_loop(0, NDP // GRP, collect_back, 0)
-        everyone(bsend.at[2 + n], brecv.at[2 + n], bsem_s, bsem_r.at[2 + n])
-    home_q(1)
+        by_z(bsend.at[2 + n], brecv.at[2 + n], bsem_s, bsem_r.at[2 + n])
+        home_q(n)
     for n, ref in enumerate((ok_ref, ov_ref)):
         pltpu.make_async_copy(brecv.at[2 + n], brecv.at[2 + n], bsem_r.at[2 + n]).wait()
         got = mm(kgather[...], brecv[2 + n].reshape(2 * ROWS, 128), 1, 0).astype(BF16)
@@ -498,10 +508,17 @@
     pltpu.make_async_copy(bsend.at[:, most], bsend.at[:, most], bsem_s).wait()
 
 
-def settle(a_ref, b_ref, c_ref, oa_ref, ob_ref, oc_ref):
-    oa_ref[...] = a_ref[...]
-    ob_ref[...] = b_ref[...]
-    oc_ref[...] = c_ref[...]
+def settle(a_ref, b_ref, c_ref, oa_ref, ob_ref, oc_ref, va, vb, vc, sin, sout):
+    ways = ((a_ref, va, oa_ref), (b_ref, vb, ob_ref), (c_ref, vc, oc_ref))
+    come = [pltpu.make_async_copy(src, mid, sin.at[n]) for n, (src, mid, _) in enumerate(ways)]
+    go = [pltpu.make_async_copy(mid, dst, sout.at[n]) for n, (_, mid, dst) in enumerate(ways)]
+    for copy in come:
+        copy.start()
+    for n in range(3):
+        come[n].wait()
+        go[n].start()
+    for copy in go:
+        copy.wait()
 
 
 def body(queries, key_rows, values, saved_out, out_grad, pack_of, segment_label):
@@ -542,7 +559,6 @@
             pltpu.VMEM((2, NDP, 6, 8, 128), BF16),
             pltpu.VMEM((2, TOK, 4 * HD), BF16),
             pltpu.VMEM((TOK, 4 * HD), BF16),
-            pltpu.VMEM((2 * ROWS, 8 * TOK), BF16),
             pltpu.VMEM((8 * TOK, 2 * ROWS), BF16),
             pltpu.VMEM((NY, 2 * 192, 128), BF16),
             pltpu.VMEM((NY, 2 * 192, 128), BF16),
@@ -563,8 +579,9 @@
     return pl.pallas_call(
         settle,
         out_shape=shapes,
-        in_specs=[pl.BlockSpec(memory_space=pltpu.VMEM)] * 3,
-        out_specs=(pl.BlockSpec(memory_space=pltpu.VMEM),) * 3,
+        in_specs=[anywhere] * 3,
+        out_specs=(anywhere,) * 3,
+        scratch_shapes=[pltpu.VMEM(shape.shape, BF16) for shape in shapes] + [dma((3,)), dma((3,))],
         name="settle",
     )(*grads)
 

time: 110 us -> 107 us (0.973); the launches traced: 110 us -> 105 us
  Pallas kernels: 110 us -> 105 us
    pallas_call x1, Pallas kernels: 107 us -> 103 us  [body(): pl.pallas_call(kernel, out_shape=shapes, in_specs=[hbm] * 7, out_specs=(a...]
where the time goes in v5:
time: 107 us; the launch traced here: 105 us
  Pallas kernels  105 us (98%)
    pallas_call x1, Pallas kernels, body(): pl.pallas_call(kernel, out_shape=shapes, in_specs=[hbm] * 7, out_specs=(a...  103 us

profile of v5, /device:TPU:1, one launch (start us, length us, event | category | flops | bytes accessed | tf_op | source)
XLA Modules:
  0.0 105.2 jit_solution(10131842185321880854)
XLA Ops:
  0.6 102.5 %packed_attention_backward.1 = (bf16[128,2048]{1,0:T(8,128)(2,1)}, bf16[128,1024]{1,0:T(8,128)(2,1)}, bf16[128,1024]{1,0:T(8,128)(2,1)}) custom-call(bf16[128,2048]{1,0:T(8,128)(2,1)} %q_ref.1, bf16[128,1024]{1,0:T(8,128)(2,1)} %k_ref.1, bf16[128,1024]{1,0:T(8,128)(2,1)} %v_ref.1, bf16[128,2048]{1,0:T(8,128)(2,1)} %g_ref.1, bf16[128,2048]{1,0:T(8,128)(2,1)} %o_ref.1, ...), custom_call_target="tpu_custom_call" | custom-call | tf_op jit(solution)/shard_map/packed_attention_backward/pallas_call | solution.py:529
  103.2 2.1 %settle.1 = (bf16[128,2048]{1,0:T(8,128)(2,1)}, bf16[128,1024]{1,0:T(8,128)(2,1)}, bf16[128,1024]{1,0:T(8,128)(2,1)}) custom-call(bf16[128,2048]{1,0:T(8,128)(2,1)} %get-tuple-element.6.a_ref, bf16[128,1024]{1,0:T(8,128)(2,1)} %get-tuple-element.7.b_ref, bf16[128,1024]{1,0:T(8,128)(2,1)} %get-tuple-element.8.c_ref), custom_call_target="tpu_custom_call" | custom-call | tf_op jit(solution)/shard_map/settle/pallas_call | solution.py:579

commit v6 on v5

--- a/solution.py
+++ b/solution.py
@@ -483,7 +483,8 @@
 
         lax.fori_loop(0, NDP // GRP, collect_back, 0)
         by_z(bsend.at[2 + n], brecv.at[2 + n], bsem_s, bsem_r.at[2 + n])
-        home_q(n)
+    home_q(0)
+    home_q(1)
     for n, ref in enumerate((ok_ref, ov_ref)):
         pltpu.make_async_copy(brecv.at[2 + n], brecv.at[2 + n], bsem_r.at[2 + n]).wait()
         got = mm(kgather[...], brecv[2 + n].reshape(2 * ROWS, 128), 1, 0).astype(BF16)

time: 107 us -> 107 us (level)
  no operation moved by 1% of the time
where the time goes in v6:
time: 107 us; the launch traced here: 105 us
  Pallas kernels  105 us (98%)
    pallas_call x1, Pallas kernels, body(): pl.pallas_call(kernel, out_shape=shapes, in_specs=[hbm] * 7, out_specs=(a...  103 us

profile of v6, /device:TPU:1, one launch (start us, length us, event | category | flops | bytes accessed | tf_op | source)
XLA Modules:
  0.0 105.2 jit_solution(9405032707695533629)
XLA Ops:
  0.6 102.5 %packed_attention_backward.1 = (bf16[128,2048]{1,0:T(8,128)(2,1)}, bf16[128,1024]{1,0:T(8,128)(2,1)}, bf16[128,1024]{1,0:T(8,128)(2,1)}) custom-call(bf16[128,2048]{1,0:T(8,128)(2,1)} %q_ref.1, bf16[128,1024]{1,0:T(8,128)(2,1)} %k_ref.1, bf16[128,1024]{1,0:T(8,128)(2,1)} %v_ref.1, bf16[128,2048]{1,0:T(8,128)(2,1)} %g_ref.1, bf16[128,2048]{1,0:T(8,128)(2,1)} %o_ref.1, ...), custom_call_target="tpu_custom_call" | custom-call | tf_op jit(solution)/shard_map/packed_attention_backward/pallas_call | solution.py:530
  103.2 2.1 %settle.1 = (bf16[128,2048]{1,0:T(8,128)(2,1)}, bf16[128,1024]{1,0:T(8,128)(2,1)}, bf16[128,1024]{1,0:T(8,128)(2,1)}) custom-call(bf16[128,2048]{1,0:T(8,128)(2,1)} %get-tuple-element.6.a_ref, bf16[128,1024]{1,0:T(8,128)(2,1)} %get-tuple-element.7.b_ref, bf16[128,1024]{1,0:T(8,128)(2,1)} %get-tuple-element.8.c_ref), custom_call_target="tpu_custom_call" | custom-call | tf_op jit(solution)/shard_map/settle/pallas_call | solution.py:580
